TPU v7x, 512 devices: a whole 4x8x8 slice. The times are simulated.
512 devices in a mesh: dp: 4 (over x), expert: 128 (over y, z, core).
Axes of the slice: x: 4, y: 8, z: 8, core: 2. Of those that a mesh axis runs over, the one named last changes fastest.
Arguments:
- embeds: bfloat16 [3, 2048, 1024], P(None, 'expert', 'dp'), may hold values from -6 to 6
- prefix_cache: bfloat16 [2048, 2, 64, 1024], P('expert', None, None, 'dp'), may hold values from -6 to 6
- w_qkv: bfloat16 [1024, 3, 1024], P(None, None, 'dp'), may hold values from -0.1875 to 0.1875
- w_up: bfloat16 [128, 1024, 2048], P('expert', None, 'dp'), may hold values from -0.1875 to 0.1875
- w_down: bfloat16 [128, 2048, 1024], P('expert', 'dp'), may hold values from -0.09375 to 0.09375
- parents: int32 [3, 2048], P(None, 'expert'), may hold values from 0 to 7
- routes: int32 [3, 2048, 2], P(None, 'expert'), may hold values from 0 to 63, all different within a row; in each aligned block of 16 rows (0 to 15, 16 to 31, ..., all dimensions but the last counted through in order) at most 2 rows name the same one
- gates: float32 [3, 2048, 2], P(None, 'expert'), may hold values from 0.2 to 1
Outputs:
- mixed: bfloat16 [3, 2048, 1024], P(None, 'expert', 'dp')
Inputs may be any that keep to these rules, and one draw needn't show every extreme that they name: `routes`: at each step the 16 rows of one device name one expert at most 2 times.
All inputs are finite; a program needn't handle non-finite values.
Results may differ from a plain program's by a relative error of at most 0.011.
Values may be sent and summed in bfloat16 or wider, within the bound.
No kernel may reach another device: no remote copies, remote signals or barrier semaphores. Data moves between devices by JAX's collectives and lax.ppermute only.
A program may use at most 64 MiB of HBM per device.

v0:
```python
import jax
import jax.numpy as jnp
from jax import lax
from jax.sharding import PartitionSpec as P

HD = 128
HALVES = 2
BEAMS = 8
PREFIX = 64
STEPS = 3


def normalize(values):
    mean_value = jnp.mean(values, axis=-1, keepdims=True)
    centred = values - mean_value
    spread = jnp.mean(centred * centred, axis=-1, keepdims=True)
    return centred * lax.rsqrt(spread + 1e-05)


def attend(query, keys, values, visible):
    number = query.shape[0]
    heads_here = query.shape[1] // HD
    length = keys.shape[1]
    query_heads = query.reshape(number, heads_here, HD)
    key_heads = keys.reshape(number, length, heads_here, HD)
    value_heads = values.reshape(number, length, heads_here, HD).astype(jnp.float32)
    scores = jnp.einsum(
        "shd,slhd->shl", query_heads, key_heads, preferred_element_type=jnp.float32
    ) * HD ** (-0.5)
    shown = jnp.arange(length) < visible
    weights = jnp.where(shown[None, None, :], jnp.exp(scores), jnp.float32(0.0))
    total = jnp.sum(weights, axis=-1)
    summed = jnp.einsum("shl,slhd->shd", weights, value_heads, precision=lax.Precision.HIGHEST)
    return (summed / total[:, :, None]).reshape(number, heads_here * HD)


def expert_layer(middle, route, gate, w_up, w_down, experts_all, capacity):
    number, shard = middle.shape
    pair_expert = route.reshape(-1)
    chosen = (pair_expert[:, None] == jnp.arange(experts_all)[None, :]).astype(jnp.int32)
    order_in = jnp.sum((jnp.cumsum(chosen, axis=0) - 1) * chosen, axis=1)
    target = pair_expert * capacity + order_in
    dispatch = (target[None, :] == jnp.arange(experts_all * capacity)[:, None]).astype(jnp.bfloat16)
    width_sent = middle.shape[1]
    pairs = jnp.repeat(middle, 2, axis=0)
    packed = jnp.dot(dispatch, pairs, preferred_element_type=jnp.float32).astype(jnp.bfloat16)
    packed = jnp.broadcast_to(
        packed.reshape(experts_all, 1, capacity, width_sent),
        (experts_all, HALVES, capacity, width_sent),
    )
    packed = packed.reshape(experts_all * HALVES, capacity, width_sent)
    whole_slots = lax.all_gather(
        lax.all_to_all(packed, "expert", split_axis=0, concat_axis=0, tiled=True),
        "dp",
        axis=2,
        tiled=True,
    )
    normed = normalize(whole_slots.astype(jnp.float32)).astype(jnp.bfloat16)
    hidden = jax.nn.relu(
        jnp.einsum("scd,df->scf", normed, w_up[0], preferred_element_type=jnp.float32)
    ).astype(jnp.bfloat16)
    half_part = jnp.einsum("scf,fd->scd", hidden, w_down[0], preferred_element_type=jnp.float32)
    share = lax.psum_scatter(half_part, "dp", scatter_dimension=2, tiled=True).astype(jnp.bfloat16)
    returned = lax.all_to_all(share, "expert", split_axis=0, concat_axis=0, tiled=True)
    merged = jnp.sum(
        returned.reshape(experts_all, HALVES, capacity, shard).astype(jnp.float32), axis=1
    )
    merged = merged.reshape(experts_all * capacity, shard)
    pair_out = jnp.dot(dispatch.astype(jnp.float32).T, merged, precision=lax.Precision.HIGHEST)
    combined = jnp.sum((pair_out * gate.reshape(-1)[:, None]).reshape(number, 2, shard), axis=1)
    return (middle.astype(jnp.float32) + combined).astype(jnp.bfloat16)


def shards(embeds, prefix_cache, w_qkv, w_up, w_down, parents, routes, gates):
    number = embeds.shape[1]
    shard = embeds.shape[2]
    width = w_qkv.shape[0]
    devices = lax.axis_size("expert")
    experts_all = devices // HALVES
    capacity = max(2, (4 * number + experts_all - 1) // experts_all)
    local_rows = jnp.arange(number, dtype=jnp.int32)
    first_beam = local_rows - local_rows % BEAMS
    joined = w_qkv.reshape(width, 3 * shard)
    history = jnp.concatenate(
        [prefix_cache, jnp.zeros((number, 2, STEPS, shard), jnp.bfloat16)], axis=2
    )
    results = []
    for step in range(STEPS):
        token = embeds[step]
        whole_row = lax.all_gather(token, "dp", axis=1, tiled=True)
        normed = normalize(whole_row.astype(jnp.float32)).astype(jnp.bfloat16)
        projected = (
            jnp.dot(normed, joined, preferred_element_type=jnp.float32)
            .astype(jnp.bfloat16)
            .reshape(number, 3, shard)
        )
        source = first_beam + parents[step]
        history = jnp.take(history, source, axis=0)
        history = history.at[:, :, PREFIX + step].set(projected[:, 1:])
        attention = attend(projected[:, 0], history[:, 0], history[:, 1], PREFIX + step + 1)
        middle = (token.astype(jnp.float32) + attention).astype(jnp.bfloat16)
        results.append(
            expert_layer(middle, routes[step], gates[step], w_up, w_down, experts_all, capacity)
        )
    return jnp.stack(results)


def solution(mesh):
    placed = (
        P(None, "expert", "dp"),
        P("expert", None, None, "dp"),
        P(None, None, "dp"),
        P("expert", None, "dp"),
        P("expert", "dp", None),
        P(None, "expert"),
        P(None, "expert", None),
        P(None, "expert", None),
    )
    return jax.shard_map(
        shards, mesh=mesh, in_specs=placed, out_specs=P(None, "expert", "dp"), check_vma=False
    )
```

profile of v0, /device:TPU:1, one launch (start us, length us, event | category | flops | bytes accessed | tf_op | source)
XLA Modules:
  0.0 271.9 jit_solution(17766300753414543734)
XLA Ops:
  8.2 1.4 compare_and_fusion
  9.6 1.3 fusion.116
  13.3 10.2 %all-gather.2 = bf16[1,16,1024]{2,1,0:T(8,128)(2,1)S(1)} all-gather(bf16[1,16,256]{2,1,0:T(8,128)(2,1)S(1)} %get-tuple-element.60), channel_id=4, replica_groups=mesh['dp'=4,'expert'=128] {'dp'}, dimensions={2}, use_global_device_ids=true | all-gather | bytes 40960 | tf_op jit(solution)/shard_map/all_gather | solution.py:90
  23.8 9.0 %all-gather = bf16[1,16,1024]{2,1,0:T(8,128)(2,1)S(1)} all-gather(bf16[1,16,256]{2,1,0:T(8,128)(2,1)S(1)} %get-tuple-element.61), channel_id=2, replica_groups=mesh['dp'=4,'expert'=128] {'dp'}, dimensions={2}, use_global_device_ids=true | all-gather | bytes 40960 | tf_op jit(solution)/shard_map/all_gather | solution.py:90
  33.2 9.0 %all-gather.1 = bf16[1,16,1024]{2,1,0:T(8,128)(2,1)S(1)} all-gather(bf16[1,16,256]{2,1,0:T(8,128)(2,1)S(1)} %get-tuple-element.62), channel_id=3, replica_groups=mesh['dp'=4,'expert'=128] {'dp'}, dimensions={2}, use_global_device_ids=true | all-gather | bytes 40960 | tf_op jit(solution)/shard_map/all_gather | solution.py:90
  42.5 1.7 copy.124
  46.5 1.3 concatenate.9
  49.6 1.1 fusion.111
  51.3 0.9 gather_fusion.1
  52.2 1.8 reshape.396
  54.7 1.0 reshape.397
  56.0 1.1 fusion.112
  57.1 0.9 gather_fusion.2
  64.1 26.3 %all-to-all-start = ((bf16[128,2,256]{2,1,0:T(2,128)(2,1)}), bf16[128,2,256]{2,1,0:T(2,128)(2,1)S(1)}, u32[]{:S(2)}, u32[]{:S(2)}) async-start(bf16[128,2,256]{2,1,0:T(2,128)(2,1)} %bitcast.10), calls=%async_computation | async-start | bytes 262144 | tf_op jit(solution)/shard_map/all_to_all | solution.py:53
  91.3 11.3 %all-to-all-done = bf16[128,2,256]{2,1,0:T(2,128)(2,1)S(1)} async-done(((bf16[128,2,256]{2,1,0:T(2,128)(2,1)}), bf16[128,2,256]{2,1,0:T(2,128)(2,1)S(1)}, u32[]{:S(2)}, u32[]{:S(2)}) %all-to-all-start) | async-done | bytes 131104 | tf_op jit(solution)/shard_map/all_to_all | solution.py:53
  103.3 6.4 %all-to-all-start.2 = ((bf16[128,2,256]{2,1,0:T(2,128)(2,1)}), bf16[128,2,256]{2,1,0:T(2,128)(2,1)S(1)}, u32[]{:S(2)}, u32[]{:S(2)}) async-start(bf16[128,2,256]{2,1,0:T(2,128)(2,1)} %bitcast.26), calls=%async_computation.3 | async-start | bytes 262144 | tf_op jit(solution)/shard_map/all_to_all | solution.py:53
  109.7 10.7 %all_gather.19 = bf16[128,2,1024]{2,1,0:T(2,128)(2,1)S(1)} all-gather(bf16[128,2,256]{2,1,0:T(2,128)(2,1)S(1)} %all-to-all-done), channel_id=1, replica_groups=mesh['dp'=4,'expert'=128] {'dp'}, dimensions={2}, use_global_device_ids=true | all-gather | bytes 655360 | tf_op jit(solution)/shard_map/all_gather | solution.py:52
  122.5 1.8 fusion.5
  124.8 9.4 %all_gather.21 = bf16[128,2,1024]{2,1,0:T(2,128)(2,1)S(1)} all-gather(bf16[128,2,256]{2,1,0:T(2,128)(2,1)S(1)} %all-to-all-done.2), channel_id=1, replica_groups=mesh['dp'=4,'expert'=128] {'dp'}, dimensions={2}, use_global_device_ids=true | all-gather | bytes 655360 | tf_op jit(solution)/shard_map/all_gather | solution.py:52
  136.1 1.8 fusion.4
  138.3 29.4 %all_to_all.30 = bf16[128,2,256]{2,1,0:T(2,128)(2,1)S(1)} all-to-all(bf16[128,2,256]{2,1,0:T(2,128)(2,1)S(1)} %bitcast.194), channel_id=1, replica_groups=mesh['dp'=4,'expert'=128] {'expert'}, dimensions={0} | all-to-all | bytes 262144 | tf_op jit(solution)/shard_map/all_to_all | solution.py:53
  167.7 16.6 %all_gather.23 = bf16[128,2,1024]{2,1,0:T(2,128)(2,1)S(1)} all-gather(bf16[128,2,256]{2,1,0:T(2,128)(2,1)S(1)} %all_to_all.30), channel_id=1, replica_groups=mesh['dp'=4,'expert'=128] {'dp'}, dimensions={2}, use_global_device_ids=true | all-gather | bytes 655360 | tf_op jit(solution)/shard_map/all_gather | solution.py:52
  186.3 1.8 fusion.3
  188.1 1.0 convert_element_type.181
  189.9 7.8 %all-to-all-start.1 = ((bf16[128,2,256]{2,1,0:T(2,128)(2,1)}), bf16[128,2,256]{2,1,0:T(2,128)(2,1)S(1)}, u32[]{:S(2)}, u32[]{:S(2)}) async-start(bf16[128,2,256]{2,1,0:T(2,128)(2,1)} %copy.132), calls=%async_computation.2 | async-start | bytes 262144 | tf_op jit(solution)/shard_map/all_to_all | solution.py:64
  198.4 1.0 convert_element_type.198
  200.1 15.9 %reduce-scatter.8.cloned.1.call-done = f32[128,2,256]{2,0,1:T(8,128)} async-done(((f32[128,2,1024]{2,0,1:T(8,128)}), f32[128,2,256]{2,0,1:T(8,128)}) %reduce-scatter.8.cloned.1.call-update) | async-done | bytes 262160 | tf_op jit(solution)/shard_map/reduce_scatter | solution.py:63
  216.0 1.0 convert_element_type.215
  217.8 15.7 %all-to-all-start.3 = ((bf16[128,2,256]{2,1,0:T(2,128)(2,1)}), bf16[128,2,256]{2,1,0:T(2,128)(2,1)S(1)}, u32[]{:S(2)}, u32[]{:S(2)}) async-start(bf16[128,2,256]{2,1,0:T(2,128)(2,1)} %copy.143), calls=%async_computation.5 | async-start | bytes 262144 | tf_op jit(solution)/shard_map/all_to_all | solution.py:64
  233.9 11.7 %all-to-all-done.3 = bf16[128,2,256]{2,1,0:T(2,128)(2,1)S(1)} async-done(((bf16[128,2,256]{2,1,0:T(2,128)(2,1)}), bf16[128,2,256]{2,1,0:T(2,128)(2,1)S(1)}, u32[]{:S(2)}, u32[]{:S(2)}) %all-to-all-start.3) | async-done | bytes 131104 | tf_op jit(solution)/shard_map/all_to_all | solution.py:64
  245.6 6.2 %all-to-all-start.5 = ((bf16[128,2,256]{2,1,0:T(2,128)(2,1)}), bf16[128,2,256]{2,1,0:T(2,128)(2,1)S(1)}, u32[]{:S(2)}, u32[]{:S(2)}) async-start(bf16[128,2,256]{2,1,0:T(2,128)(2,1)} %copy.154), calls=%async_computation.8 | async-start | bytes 262144 | tf_op jit(solution)/shard_map/all_to_all | solution.py:64
  252.5 11.7 %all-to-all-done.5 = bf16[128,2,256]{2,1,0:T(2,128)(2,1)S(1)} async-done(((bf16[128,2,256]{2,1,0:T(2,128)(2,1)}), bf16[128,2,256]{2,1,0:T(2,128)(2,1)S(1)}, u32[]{:S(2)}, u32[]{:S(2)}) %all-to-all-start.5) | async-done | bytes 131104 | tf_op jit(solution)/shard_map/all_to_all | solution.py:64
  (185 shorter events, 29.9 us)
Async XLA Ops:
  6.5 115.9 %copy-start = (bf16[1,512,1024]{2,1,0:T(8,128)(2,1)S(1)}, bf16[1,512,1024]{2,1,0:T(8,128)(2,1)}, u32[]{:S(2)}) copy-start(bf16[1,512,1024]{2,1,0:T(8,128)(2,1)} %param.20) | copy-start | bytes 3145732
  45.9 0.6 copy-start.7
  49.6 1.1 copy-start.15
  49.6 1.1 copy-start.16
  51.3 2.7 %copy-start.8 = (bf16[16,3,256]{2,1,0:T(4,128)(2,1)S(1)}, bf16[16,3,256]{2,1,0:T(4,128)(2,1)}, u32[]{:S(2)}) copy-start(bf16[16,3,256]{2,1,0:T(4,128)(2,1)} %copy-done.7) | copy-start | bytes 73732
  52.2 2.3 copy-start.19
  52.2 2.5 copy-start.5
  54.5 1.2 copy-start.14
  57.1 0.9 copy-start.13
  58.3 1.1 copy-start.4
  58.5 1.5 copy-start.18
  58.5 1.6 copy-start.17
  58.6 1.8 copy-start.3
  60.0 1.1 copy-start.2
  60.8 2.4 copy-start.6
  60.8 2.5 copy-start.12
  61.7 28.7 %copy-start.10 = (s32[1,16,2]{1,2,0:T(2,128)S(1)}, s32[1,16,2]{1,2,0:T(2,128)}, u32[]{:S(2)}) copy-start(s32[1,16,2]{1,2,0:T(2,128)} %get-tuple-element.74) | copy-start | bytes 388
  61.7 29.3 %copy-start.9 = (s32[1,16,2]{1,2,0:T(2,128)S(1)}, s32[1,16,2]{1,2,0:T(2,128)}, u32[]{:S(2)}) copy-start(s32[1,16,2]{1,2,0:T(2,128)} %get-tuple-element.73) | copy-start | bytes 388
  64.1 38.5 %all-to-all-start = ((bf16[128,2,256]{2,1,0:T(2,128)(2,1)}), bf16[128,2,256]{2,1,0:T(2,128)(2,1)S(1)}, u32[]{:S(2)}, u32[]{:S(2)}) async-start(bf16[128,2,256]{2,1,0:T(2,128)(2,1)} %bitcast.10), calls=%async_computation | async-start | bytes 262144 | tf_op jit(solution)/shard_map/all_to_all | solution.py:53
  103.3 21.5 %all-to-all-start.2 = ((bf16[128,2,256]{2,1,0:T(2,128)(2,1)}), bf16[128,2,256]{2,1,0:T(2,128)(2,1)S(1)}, u32[]{:S(2)}, u32[]{:S(2)}) async-start(bf16[128,2,256]{2,1,0:T(2,128)(2,1)} %bitcast.26), calls=%async_computation.3 | async-start | bytes 262144 | tf_op jit(solution)/shard_map/all_to_all | solution.py:53
  109.7 78.4 %reduce-scatter.4.cloned.1.call-start = ((), (), s32[]{:S(2)}) async-start(), calls=%async_computation.9 | async-start | bytes 1310720 | tf_op jit(solution)/shard_map/reduce_scatter | solution.py:63
  121.0 1.5 copy-start.1
  124.4 74.0 %reduce-scatter.6.cloned.1.call-start = ((), (), s32[]{:S(2)}) async-start(), calls=%async_computation.10 | async-start | bytes 1310720 | tf_op jit(solution)/shard_map/reduce_scatter | solution.py:63
  137.9 78.1 %reduce-scatter.8.cloned.1.call-start = ((), (), s32[]{:S(2)}) async-start(), calls=%async_computation.11 | async-start | bytes 1310720 | tf_op jit(solution)/shard_map/reduce_scatter | solution.py:63
  188.1 9.7 %copy-start.11 = (f32[3,16,2]{1,2,0:T(2,128)S(1)}, f32[3,16,2]{1,2,0:T(2,128)}, u32[]{:S(2)}) copy-start(f32[3,16,2]{1,2,0:T(2,128)} %param.23) | copy-start | bytes 1156
  189.9 27.9 %all-to-all-start.1 = ((bf16[128,2,256]{2,1,0:T(2,128)(2,1)}), bf16[128,2,256]{2,1,0:T(2,128)(2,1)S(1)}, u32[]{:S(2)}, u32[]{:S(2)}) async-start(bf16[128,2,256]{2,1,0:T(2,128)(2,1)} %copy.132), calls=%async_computation.2 | async-start | bytes 262144 | tf_op jit(solution)/shard_map/all_to_all | solution.py:64
  217.8 27.9 %all-to-all-start.3 = ((bf16[128,2,256]{2,1,0:T(2,128)(2,1)}), bf16[128,2,256]{2,1,0:T(2,128)(2,1)S(1)}, u32[]{:S(2)}, u32[]{:S(2)}) async-start(bf16[128,2,256]{2,1,0:T(2,128)(2,1)} %copy.143), calls=%async_computation.5 | async-start | bytes 262144 | tf_op jit(solution)/shard_map/all_to_all | solution.py:64
  245.6 18.5 %all-to-all-start.5 = ((bf16[128,2,256]{2,1,0:T(2,128)(2,1)}), bf16[128,2,256]{2,1,0:T(2,128)(2,1)S(1)}, u32[]{:S(2)}, u32[]{:S(2)}) async-start(bf16[128,2,256]{2,1,0:T(2,128)(2,1)} %copy.154), calls=%async_computation.8 | async-start | bytes 262144 | tf_op jit(solution)/shard_map/all_to_all | solution.py:64
Sparse Core Ops, SparseCore 0:
  124.5 28.1 reduce-scatter.3
  155.8 32.1 reduce-scatter.5
  190.8 25.1 reduce-scatter.7
where the time goes:
time: 273 us; the launch traced here: 272 us
  blocking collectives  94.4 us (35%)
  starting transfers between devices  62.4 us (23%)
  waiting for transfers between devices  50.7 us (19%)
  local copies, waits for them, and re-layouts  20.9 us (8%)
  other arithmetic  18.5 us (7%)
  between operations  13.9 us (5%)
  matrix products  11.1 us (4%)
    all_gather x3, blocking collectives, expert_layer(): lax.all_gather(lax.all_to_all(packed, 'expert', split_axis=0, concat_axis...  36.7 us
    all_to_all x2, starting transfers between devices, expert_layer(): lax.all_to_all(packed, 'expert', split_axis=0, concat_axis=0, tiled=True)  32.6 us
    all_to_all x3, starting transfers between devices, expert_layer(): lax.all_to_all(share, 'expert', split_axis=0, concat_axis=0, tiled=True)  29.7 us
    all_to_all x1, blocking collectives, expert_layer(): lax.all_to_all(packed, 'expert', split_axis=0, concat_axis=0, tiled=True)  29.4 us
    all_gather x3, blocking collectives, shards(): whole_row = lax.all_gather(token, 'dp', axis=1, tiled=True)  28.2 us
    all_to_all x3, waiting for transfers between devices, expert_layer(): lax.all_to_all(share, 'expert', split_axis=0, concat_axis=0, tiled=True)  23.4 us
    reduce_scatter x3, waiting for transfers between devices, expert_layer(): lax.psum_scatter(half_part, 'dp', scatter_dimension=2, tiled=True)  15.9 us
    all_to_all x2, waiting for transfers between devices, expert_layer(): lax.all_to_all(packed, 'expert', split_axis=0, concat_axis=0, tiled=True)  11.3 us
  transfers between devices with their start and end apart: 8, of which 4 were waited for; matrix products, arithmetic and copies ran while one was open for 7% of the time, Pallas kernels for 0%

commit v1 on v0

v1 whole, which is shorter than its diff:
```python
import functools

import jax
import jax.numpy as jnp
from jax import lax
from jax.experimental import pallas as pl
from jax.experimental.pallas import tpu as pltpu
from jax.sharding import Mesh
from jax.sharding import PartitionSpec as P

HD = 128
CORES = 2
BEAMS = 8
CAP = 2
PAD = 8
HIDE = -1e30
F32 = jnp.float32
BF16 = jnp.bfloat16


def iota(shape, dim):
    return lax.broadcasted_iota(jnp.int32, shape, dim)


def dot(a, b):
    return jnp.dot(a, b, preferred_element_type=F32)


def dot_last(a, b):
    return lax.dot_general(a, b, (((1,), (1,)), ((), ())), preferred_element_type=F32)


def call(kernel, outs, *args, cost=None):
    flops, nbytes = cost or (0, 0)
    return pl.pallas_call(
        kernel,
        out_shape=outs,
        in_specs=[pl.BlockSpec(memory_space=pltpu.VMEM)] * len(args),
        out_specs=jax.tree.map(lambda _: pl.BlockSpec(memory_space=pltpu.VMEM), outs),
        compiler_params=pltpu.CompilerParams(vmem_limit_bytes=32 * 1024 * 1024),
        cost_estimate=pl.CostEstimate(flops=flops, bytes_accessed=nbytes, transcendentals=0),
    )(*args)


def plan_kernel(rows, steps, prefix, experts, parents_ref, route_row_ref, route_col_ref, gate_ref, bias_ref, pack_ref, high_ref, low_ref):
    total = rows * steps
    local = iota((rows, 1), 0)
    first = local - local % BEAMS
    parent = [
        (iota((rows, rows), 1) == first + parents_ref[t * rows : (t + 1) * rows, :]).astype(F32).astype(BF16)
        for t in range(steps)
    ]
    eye = (iota((rows, rows), 0) == iota((rows, rows), 1)).astype(F32)
    none = jnp.zeros((rows, rows), F32)
    origin = []
    seen = []
    for t in range(steps):
        if t == 0:
            origin.append(parent[0].astype(F32))
            seen.append([eye] + [none] * (steps - 1))
        else:
            origin.append(dot(parent[t], origin[t - 1].astype(BF16)))
            seen.append([dot(parent[t], seen[t - 1][s].astype(BF16)) for s in range(t)] + [eye] + [none] * (steps - 1 - t))
    spread = (iota((rows, rows * prefix), 1) // prefix == iota((rows, rows * prefix), 0)).astype(F32).astype(BF16)
    old = dot(jnp.concatenate(origin, axis=0).astype(BF16), spread)
    bias_ref[:, : rows * prefix] = jnp.where(old > 0.5, 0.0, HIDE)
    new = jnp.concatenate([jnp.concatenate(seen[t], axis=1) for t in range(steps)], axis=0)
    bias_ref[:, rows * prefix :] = jnp.full((total, HD), HIDE, F32)
    bias_ref[:, rows * prefix : rows * prefix + total] = jnp.where(new > 0.5, 0.0, HIDE)

    a, b = iota((total, total), 0), iota((total, total), 1)
    same = a // rows == b // rows
    before = (same & (b < a)).astype(F32).astype(BF16)
    after = (same & (a < b)).astype(F32).astype(BF16)
    named = [(iota((total, experts), 1) == route_col_ref[:, k : k + 1]).astype(F32) for k in range(2)]
    count = dot(before, (named[0] + named[1]).astype(BF16))
    step_at = (iota((total, 1), 0) // rows) * CAP
    weights = jnp.zeros((total, experts * PAD), F32)
    for k in range(2):
        order = jnp.sum(named[k] * count, axis=1, keepdims=True).astype(jnp.int32)
        target = route_col_ref[:, k : k + 1] * PAD + step_at + order
        weights += jnp.where(iota((total, experts * PAD), 1) == target, gate_ref[:, k : k + 1], 0.0)
    high = weights.astype(BF16)
    high_ref[...] = high
    low_ref[...] = (weights - high.astype(F32)).astype(BF16)

    named = [(iota((experts, total), 0) == route_row_ref[k : k + 1, :]).astype(F32) for k in range(2)]
    count = dot((named[0] + named[1]).astype(BF16), after)
    step_at = (iota((1, total), 1) // rows) * CAP
    chosen = jnp.zeros((experts * PAD, total), F32)
    for k in range(2):
        order = jnp.sum(named[k] * count, axis=0, keepdims=True).astype(jnp.int32)
        target = route_row_ref[k : k + 1, :] * PAD + step_at + order
        chosen += (iota((experts * PAD, total), 0) == target).astype(F32)
    pack_ref[...] = chosen.astype(BF16)


def normed_blocks(blocks):
    width = sum(v.shape[-1] for v in blocks)
    mean = sum(jnp.sum(v, axis=-1, keepdims=True) for v in blocks) / width
    centred = [v - mean for v in blocks]
    spread = sum(jnp.sum(v * v, axis=-1, keepdims=True) for v in centred) / width
    scale = lax.rsqrt(spread + 1e-05)
    return jnp.concatenate([(v * scale).astype(BF16) for v in centred], axis=-1)


def attend_kernel(prefix, gathered_ref, token_ref, w_ref, cache_ref, bias_ref, pack_ref, middle_ref, packed_ref):
    parts = gathered_ref.shape[0]
    total, shard = token_ref.shape
    rows = cache_ref.shape[0]
    normed = normed_blocks([gathered_ref[i].astype(F32) for i in range(parts)])
    query, key, value = (dot(normed, w_ref[j]).astype(BF16) for j in range(3))
    bias_old = bias_ref[:, : rows * prefix]
    bias_new = bias_ref[:, rows * prefix : rows * prefix + total]
    for h in range(shard // HD):
        at = slice(h * HD, (h + 1) * HD)
        old_keys = cache_ref[:, 0, :, at].reshape(rows * prefix, HD)
        old_values = cache_ref[:, 1, :, at].reshape(rows * prefix, HD)
        w_old = jnp.exp(dot_last(query[:, at], old_keys) * HD ** (-0.5) + bias_old)
        w_new = jnp.exp(dot_last(query[:, at], key[:, at]) * HD ** (-0.5) + bias_new)
        weight = jnp.sum(w_old, axis=-1, keepdims=True) + jnp.sum(w_new, axis=-1, keepdims=True)
        summed = dot(w_old.astype(BF16), old_values) + dot(w_new.astype(BF16), value[:, at])
        middle_ref[:, at] = (token_ref[:, at].astype(F32) + summed / weight).astype(BF16)
    packed_ref[...] = dot(pack_ref[...], middle_ref[...]).astype(BF16)


def spread_kernel(used, arrived_ref, out_ref):
    group = 8
    keep = (iota((group * used, group * PAD), 1) == (iota((group * used, 1), 0) // used) * PAD + iota((group * used, 1), 0) % used)
    keep = keep.astype(F32).astype(BF16)
    for g in range(arrived_ref.shape[0] // (group * PAD)):
        block = dot(keep, arrived_ref[g * group * PAD : (g + 1) * group * PAD, :]).astype(BF16)
        for i in range(out_ref.shape[0]):
            out_ref[i, g * group * used : (g + 1) * group * used, :] = block


def expert_kernel(slots_ref, up_ref, up_other_ref, down_ref, down_other_ref, out_ref):
    parts, slots, shard = slots_ref.shape
    block = slots // 3
    for g in range(slots // block):
        at = slice(g * block, (g + 1) * block)
        normed = normed_blocks([slots_ref[i, at, :].astype(F32) for i in range(parts)])
        hidden = jax.nn.relu(dot(normed, up_ref[0])).astype(BF16)
        hidden_other = jax.nn.relu(dot(normed, up_other_ref[0])).astype(BF16)
        piece = dot(hidden, down_ref[0]) + dot(hidden_other, down_other_ref[0])
        for i in range(parts):
            out_ref[i, at, :] = piece[:, i * shard : (i + 1) * shard].astype(BF16)


def sum_kernel(used, parts_ref, out_ref):
    group = 8
    place = (iota((group * PAD, group * used), 0) == (iota((1, group * used), 1) // used) * PAD + iota((1, group * used), 1) % used)
    place = place.astype(F32).astype(BF16)
    for g in range(out_ref.shape[0] // (group * PAD)):
        at = slice(g * group * used, (g + 1) * group * used)
        total = sum(parts_ref[i, at, :].astype(F32) for i in range(parts_ref.shape[0]))
        out_ref[g * group * PAD : (g + 1) * group * PAD, :] = dot(place, total.astype(BF16)).astype(BF16)


def combine_kernel(middle_ref, returned_ref, high_ref, low_ref, out_ref):
    returned = returned_ref[...]
    added = dot(high_ref[...], returned) + dot(low_ref[...], returned)
    out_ref[...] = (middle_ref[...].astype(F32) + added).astype(BF16)


def shards(parts, experts, embeds, prefix_cache, w_qkv, w_up, w_down, parents, routes, gates):
    steps, rows, shard = embeds.shape
    width = w_qkv.shape[0]
    prefix = prefix_cache.shape[2]
    total = steps * rows
    used = steps * CAP
    slots = experts * used
    shape = jax.ShapeDtypeStruct

    def exchange(values, axis):
        return lax.all_to_all(values, axis, split_axis=0, concat_axis=0, tiled=True)

    tokens = embeds.reshape(total, shard)
    gathered = exchange(jnp.broadcast_to(tokens[None], (parts, total, shard)), "x")
    swap = [(i, (i + 1) % CORES) for i in range(CORES)]
    up_other = lax.ppermute(w_up, "core", swap)
    down_other = lax.ppermute(w_down, "core", swap)
    bias, pack, high, low = call(
        functools.partial(plan_kernel, rows, steps, prefix, experts),
        (
            shape((total, rows * prefix + HD), F32),
            shape((experts * PAD, total), BF16),
            shape((total, experts * PAD), BF16),
            shape((total, experts * PAD), BF16),
        ),
        parents.reshape(total, 1),
        routes.transpose(2, 0, 1).reshape(2, total),
        routes.reshape(total, 2),
        gates.reshape(total, 2),
        cost=(10**8, 10**6),
    )
    middle, packed = call(
        functools.partial(attend_kernel, prefix),
        (shape((total, shard), BF16), shape((experts * PAD, shard), BF16)),
        gathered,
        tokens,
        w_qkv.transpose(1, 0, 2),
        prefix_cache,
        bias,
        pack,
        cost=(2 * total * width * 3 * shard, 3 * 10**6),
    )
    arrived = exchange(packed.reshape(experts, PAD, shard), "yz").reshape(experts * PAD, shard)
    spread = call(functools.partial(spread_kernel, used), shape((parts, slots, shard), BF16), arrived)
    whole = exchange(spread, "x")
    share = call(
        expert_kernel,
        shape((parts, slots, shard), BF16),
        whole,
        w_up,
        up_other,
        w_down,
        down_other,
        cost=(8 * slots * width * w_up.shape[2], 6 * 10**6),
    )
    pieces = exchange(share, "x")
    summed = call(functools.partial(sum_kernel, used), shape((experts * PAD, shard), BF16), pieces)
    returned = exchange(summed.reshape(experts, PAD, shard), "yz").reshape(experts * PAD, shard)
    mixed = call(combine_kernel, shape((total, shard), BF16), middle, returned, high, low)
    return mixed.reshape(steps, rows, shard)


def solution(mesh):
    parts, devices = mesh.shape["dp"], mesh.shape["expert"]
    experts = devices // CORES
    split = Mesh(mesh.devices.reshape(parts, experts, CORES), ("x", "yz", "core"))
    rows = ("yz", "core")
    placed = (
        P(None, rows, "x"),
        P(rows, None, None, "x"),
        P(None, None, "x"),
        P(rows, None, "x"),
        P(rows, "x", None),
        P(None, rows),
        P(None, rows, None),
        P(None, rows, None),
    )
    return jax.shard_map(
        functools.partial(shards, parts, experts), mesh=split, in_specs=placed, out_specs=P(None, rows, "x"), check_vma=False
    )
```

time: 273 us -> 99.6 us (0.36)
  the two profiles are of different devices: /device:TPU:1 before, /device:TPU:2 now
where the time goes in v1:
time: 99.6 us; the launch traced here: 98.8 us
  blocking collectives  33.4 us (34%)
  starting transfers between devices  30.4 us (31%)
  waiting for transfers between devices  18.4 us (18%)
  Pallas kernels  8.72 us (9%)
  local copies, waits for them, and re-layouts  7.83 us (8%)
    all_to_all x2, blocking collectives, exchange(): return lax.all_to_all(values, axis, split_axis=0, concat_axis=0, tiled=True)  33.4 us
    all_to_all x3, starting transfers between devices, exchange(): return lax.all_to_all(values, axis, split_axis=0, concat_axis=0, tiled=True)  26.1 us
    all_to_all x3, waiting for transfers between devices, exchange(): return lax.all_to_all(values, axis, split_axis=0, concat_axis=0, tiled=True)  18.4 us
    pallas_call x6, Pallas kernels, call(): pl.pallas_call(kernel, out_shape=outs, in_specs=[pl.BlockSpec(memory_spac...  8.72 us
    unnamed x10, local copies, waits for them, and re-layouts  3.38 us
    ppermute x1, starting transfers between devices, shards(): down_other = lax.ppermute(w_down, 'core', swap)  2.41 us
  transfers between devices with their start and end apart: 5, of which 3 were waited for; matrix products, arithmetic and copies ran while one was open for 3% of the time, Pallas kernels for 2%

profile of v1, /device:TPU:2, one launch (start us, length us, event | category | flops | bytes accessed | tf_op | source)
XLA Modules:
  0.0 98.8 jit_solution(15941325873705748615)
XLA Ops:
  0.0 1.4 %broadcast_in_dim.8 = bf16[4,48,256]{2,1,0:T(8,128)(2,1)} broadcast(bf16[48,256]{1,0:T(8,128)(2,1)} %bitcast.14), dimensions={1,2} | broadcast | bytes 122880 | tf_op jit(solution)/shard_map/broadcast_in_dim | solution.py:179
  1.4 9.2 %all-to-all-start = ((bf16[4,48,256]{2,1,0:T(8,128)(2,1)}), bf16[4,48,256]{2,1,0:T(8,128)(2,1)S(1)}, u32[]{:S(2)}, u32[]{:S(2)}) async-start(bf16[4,48,256]{2,1,0:T(8,128)(2,1)} %broadcast_in_dim.8), calls=%async_computation | async-start | bytes 196608 | tf_op jit(solution)/shard_map/all_to_all | solution.py:176
  10.6 0.8 copy.21
  11.3 0.7 copy.15
  12.0 0.1 reshape.30.route_row_ref
  12.1 0.8 reshape.38.parents_ref
  12.9 0.8 copy.22
  13.6 0.7 shard_map.82
  14.3 0.6 all-to-all-done.gathered_ref
  14.9 0.0 copy-start
  14.9 1.4 %copy-done = bf16[1024,3,256]{2,0,1:T(8,128)(2,1)S(1)} copy-done((bf16[1024,3,256]{2,0,1:T(8,128)(2,1)S(1)}, bf16[1024,3,256]{2,0,1:T(8,128)(2,1)}, u32[]{:S(2)}) %copy-start) | copy-done | bytes 1572888
  16.3 0.0 copy-start.1
  16.3 1.2 %copy-done.1 = bf16[16,2,64,256]{3,2,1,0:T(8,128)(2,1)S(1)} copy-done((bf16[16,2,64,256]{3,2,1,0:T(8,128)(2,1)S(1)}, bf16[16,2,64,256]{3,2,1,0:T(8,128)(2,1)}, u32[]{:S(2)}) %copy-start.1) | copy-done | bytes 1048600
  17.5 0.0 copy-start.2
  17.5 0.7 copy-done.2
  18.3 1.9 %shard_map.83 = (bf16[48,256]{1,0:T(8,128)(2,1)S(1)}, bf16[512,256]{1,0:T(8,128)(2,1)}) custom-call(bf16[4,48,256]{2,1,0:T(8,128)(2,1)S(1)} %all-to-all-done.gathered_ref, bf16[48,256]{1,0:T(8,128)(2,1)S(1)} %bitcast.15, bf16[3,1024,256]{2,1,0:T(8,128)(2,1)S(1)} %bitcast.10, bf16[16,2,64,256]{3,2,1,0:T(8,128)(2,1)S(1)} %copy-done.1, ...), custom_call_target="tpu_custom_call" | custom-call | flops 75497472 | bytes 3000000 | tf_op jit(solution)/shard_map/pallas_call | solution.py:35
  20.2 12.2 %all-to-all-start.1 = ((bf16[64,8,256]{2,1,0:T(8,128)(2,1)}), bf16[64,8,256]{2,1,0:T(8,128)(2,1)S(1)}, u32[]{:S(2)}, u32[]{:S(2)}) async-start(bf16[64,8,256]{2,1,0:T(8,128)(2,1)} %bitcast.5), calls=%async_computation.1 | async-start | bytes 524288 | tf_op jit(solution)/shard_map/all_to_all | solution.py:176
  32.5 0.0 copy-done.3
  32.5 1.9 %collective-permute-start = (bf16[1,1024,512]{2,1,0:T(8,128)(2,1)S(1)}, bf16[1,1024,512]{2,1,0:T(8,128)(2,1)}, u32[]{:S(2)}, u32[]{:S(2)}) collective-permute-start(bf16[1,1024,512]{2,1,0:T(8,128)(2,1)S(1)} %copy-done.3), channel_id=1, source_target_pairs={{0,1},{1,0},{2,3},{3,2},{4,5},{5,4},{6,7},{7,6},{8,9},{9,8},{10,11... | collective-permute-start | bytes 3145736 | tf_op jit(solution)/shard_map/ppermute | solution.py:181
  34.4 0.0 copy-done.4
  34.4 2.4 %collective-permute-start.1 = (bf16[1,512,1024]{2,1,0:T(8,128)(2,1)S(1)}, bf16[1,512,1024]{2,1,0:T(8,128)(2,1)}, u32[]{:S(2)}, u32[]{:S(2)}) collective-permute-start(bf16[1,512,1024]{2,1,0:T(8,128)(2,1)S(1)} %copy-done.4), channel_id=1, source_target_pairs={{0,1},{1,0},{2,3},{3,2},{4,5},{5,4},{6,7},{7,6},{8,9},{9,8},{10,11... | collective-permute-start | bytes 3145736 | tf_op jit(solution)/shard_map/ppermute | solution.py:182
  36.8 9.6 %all-to-all-done.1 = bf16[64,8,256]{2,1,0:T(8,128)(2,1)S(1)} async-done(((bf16[64,8,256]{2,1,0:T(8,128)(2,1)}), bf16[64,8,256]{2,1,0:T(8,128)(2,1)S(1)}, u32[]{:S(2)}, u32[]{:S(2)}) %all-to-all-start.1) | async-done | bytes 262176 | tf_op jit(solution)/shard_map/all_to_all | solution.py:176
  46.5 1.1 %shard_map.84 = bf16[4,384,256]{2,1,0:T(8,128)(2,1)} custom-call(bf16[512,256]{1,0:T(8,128)(2,1)S(1)} %bitcast.12), custom_call_target="tpu_custom_call" | custom-call | tf_op jit(solution)/shard_map/pallas_call | solution.py:35
  47.6 4.7 %all-to-all-start.2 = ((bf16[4,384,256]{2,1,0:T(8,128)(2,1)}), bf16[4,384,256]{2,1,0:T(8,128)(2,1)S(1)}, u32[]{:S(2)}, u32[]{:S(2)}) async-start(bf16[4,384,256]{2,1,0:T(8,128)(2,1)} %shard_map.84), calls=%async_computation.2 | async-start | bytes 1572864 | tf_op jit(solution)/shard_map/all_to_all | solution.py:176
  52.2 0.0 collective-permute-done.up_other_ref
  52.2 0.0 collective-permute-done.1.down_other_ref
  52.3 8.2 %all-to-all-done.2.slots_ref = bf16[4,384,256]{2,1,0:T(8,128)(2,1)S(1)} async-done(((bf16[4,384,256]{2,1,0:T(8,128)(2,1)}), bf16[4,384,256]{2,1,0:T(8,128)(2,1)S(1)}, u32[]{:S(2)}, u32[]{:S(2)}) %all-to-all-start.2) | async-done | bytes 786464 | tf_op jit(solution)/shard_map/all_to_all | solution.py:176
  60.4 3.9 %shard_map.85 = bf16[4,384,256]{2,1,0:T(8,128)(2,1)S(1)} custom-call(bf16[4,384,256]{2,1,0:T(8,128)(2,1)S(1)} %all-to-all-done.2.slots_ref, bf16[1,1024,512]{2,1,0:T(8,128)(2,1)S(1)} %copy-done.3, bf16[1,1024,512]{2,1,0:T(8,128)(2,1)} %collective-permute-done.up_other_ref, bf16[1,512,1024]{2,1,0:T(8,128)(2,1)S(1)} %copy-done.4, ...), custom_call_target="tpu_custom_call" | custom-call | flops 1610612736 | bytes 6000000 | tf_op jit(solution)/shard_map/pallas_call | solution.py:35
  64.3 11.9 %all_to_all.25.parts_ref = bf16[4,384,256]{2,1,0:T(8,128)(2,1)S(1)} all-to-all(bf16[4,384,256]{2,1,0:T(8,128)(2,1)S(1)} %shard_map.85), channel_id=1, replica_groups=mesh['x'=4,'yz'=64,'core'=2] {'x'}, dimensions={0} | all-to-all | bytes 1572864 | tf_op jit(solution)/shard_map/all_to_all | solution.py:176
  76.2 0.3 shard_map.86
  76.5 21.5 %all_to_all.26 = bf16[64,8,256]{2,1,0:T(8,128)(2,1)S(1)} all-to-all(bf16[64,8,256]{2,1,0:T(8,128)(2,1)S(1)} %bitcast.13), channel_id=1, replica_groups=mesh['x'=4,'yz'=64,'core'=2] {'yz'}, dimensions={0} | all-to-all | bytes 524288 | tf_op jit(solution)/shard_map/all_to_all | solution.py:176
  98.0 0.8 shard_map.87
  (2 shorter events, 0.0 us)
Async XLA Ops:
  1.4 13.5 %all-to-all-start = ((bf16[4,48,256]{2,1,0:T(8,128)(2,1)}), bf16[4,48,256]{2,1,0:T(8,128)(2,1)S(1)}, u32[]{:S(2)}, u32[]{:S(2)}) async-start(bf16[4,48,256]{2,1,0:T(8,128)(2,1)} %broadcast_in_dim.8), calls=%async_computation | async-start | bytes 196608 | tf_op jit(solution)/shard_map/all_to_all | solution.py:176
  14.9 1.4 %copy-start = (bf16[1024,3,256]{2,0,1:T(8,128)(2,1)S(1)}, bf16[1024,3,256]{2,0,1:T(8,128)(2,1)}, u32[]{:S(2)}) copy-start(bf16[1024,3,256]{2,0,1:T(8,128)(2,1)} %param.10) | copy-start | bytes 4718596
  16.3 1.2 %copy-start.1 = (bf16[16,2,64,256]{3,2,1,0:T(8,128)(2,1)S(1)}, bf16[16,2,64,256]{3,2,1,0:T(8,128)(2,1)}, u32[]{:S(2)}) copy-start(bf16[16,2,64,256]{3,2,1,0:T(8,128)(2,1)} %cache_ref.1) | copy-start | bytes 3145732
  17.5 0.7 copy-start.2
  18.3 14.2 %copy-start.3 = (bf16[1,1024,512]{2,1,0:T(8,128)(2,1)S(1)}, bf16[1,1024,512]{2,1,0:T(8,128)(2,1)}, u32[]{:S(2)}) copy-start(bf16[1,1024,512]{2,1,0:T(8,128)(2,1)} %up_ref.1) | copy-start | bytes 3145732
  18.3 16.1 %copy-start.4 = (bf16[1,512,1024]{2,1,0:T(8,128)(2,1)S(1)}, bf16[1,512,1024]{2,1,0:T(8,128)(2,1)}, u32[]{:S(2)}) copy-start(bf16[1,512,1024]{2,1,0:T(8,128)(2,1)} %down_ref.1) | copy-start | bytes 3145732
  20.2 26.2 %all-to-all-start.1 = ((bf16[64,8,256]{2,1,0:T(8,128)(2,1)}), bf16[64,8,256]{2,1,0:T(8,128)(2,1)S(1)}, u32[]{:S(2)}, u32[]{:S(2)}) async-start(bf16[64,8,256]{2,1,0:T(8,128)(2,1)} %bitcast.5), calls=%async_computation.1 | async-start | bytes 524288 | tf_op jit(solution)/shard_map/all_to_all | solution.py:176
  32.5 19.8 %collective-permute-start = (bf16[1,1024,512]{2,1,0:T(8,128)(2,1)S(1)}, bf16[1,1024,512]{2,1,0:T(8,128)(2,1)}, u32[]{:S(2)}, u32[]{:S(2)}) collective-permute-start(bf16[1,1024,512]{2,1,0:T(8,128)(2,1)S(1)} %copy-done.3), channel_id=1, source_target_pairs={{0,1},{1,0},{2,3},{3,2},{4,5},{5,4},{6,7},{7,6},{8,9},{9,8},{10,11... | collective-permute-start | bytes 3145736 | tf_op jit(solution)/shard_map/ppermute | solution.py:181
  34.4 17.8 %collective-permute-start.1 = (bf16[1,512,1024]{2,1,0:T(8,128)(2,1)S(1)}, bf16[1,512,1024]{2,1,0:T(8,128)(2,1)}, u32[]{:S(2)}, u32[]{:S(2)}) collective-permute-start(bf16[1,512,1024]{2,1,0:T(8,128)(2,1)S(1)} %copy-done.4), channel_id=1, source_target_pairs={{0,1},{1,0},{2,3},{3,2},{4,5},{5,4},{6,7},{7,6},{8,9},{9,8},{10,11... | collective-permute-start | bytes 3145736 | tf_op jit(solution)/shard_map/ppermute | solution.py:182
  47.6 12.9 %all-to-all-start.2 = ((bf16[4,384,256]{2,1,0:T(8,128)(2,1)}), bf16[4,384,256]{2,1,0:T(8,128)(2,1)S(1)}, u32[]{:S(2)}, u32[]{:S(2)}) async-start(bf16[4,384,256]{2,1,0:T(8,128)(2,1)} %shard_map.84), calls=%async_computation.2 | async-start | bytes 1572864 | tf_op jit(solution)/shard_map/all_to_all | solution.py:176

commit v2 on v1

--- a/solution.py
+++ b/solution.py
@@ -30,27 +30,47 @@
     return lax.dot_general(a, b, (((1,), (1,)), ((), ())), preferred_element_type=F32)
 
 
-def call(kernel, outs, *args, cost=None):
+def call(kernel, outs, *args, cost=None, in_hbm=(), scratch=()):
     flops, nbytes = cost or (0, 0)
     return pl.pallas_call(
         kernel,
         out_shape=outs,
-        in_specs=[pl.BlockSpec(memory_space=pltpu.VMEM)] * len(args),
+        in_specs=[pl.BlockSpec(memory_space=pl.ANY if i in in_hbm else pltpu.VMEM) for i in range(len(args))],
         out_specs=jax.tree.map(lambda _: pl.BlockSpec(memory_space=pltpu.VMEM), outs),
-        compiler_params=pltpu.CompilerParams(vmem_limit_bytes=32 * 1024 * 1024),
+        scratch_shapes=scratch,
+        compiler_params=pltpu.CompilerParams(vmem_limit_bytes=16 * 1024 * 1024),
         cost_estimate=pl.CostEstimate(flops=flops, bytes_accessed=nbytes, transcendentals=0),
     )(*args)
 
 
-def plan_kernel(rows, steps, prefix, experts, parents_ref, route_row_ref, route_col_ref, gate_ref, bias_ref, pack_ref, high_ref, low_ref):
+def plan_kernel(
+    rows, steps, prefix, experts, first_expert,
+    parents_ref, route_ref, gate_ref, w_hbm, cache_hbm, up_hbm, down_hbm,
+    bias_ref, pack_ref, high_ref, low_ref, w_ref, cache_ref, expert_ref, sems,
+):
+    half = up_hbm.shape[1] // 2
+    hidden = up_hbm.shape[2]
+    copies = [
+        pltpu.make_async_copy(up_hbm.at[0, :half, :], expert_ref.at[:, :hidden], sems.at[0]),
+        pltpu.make_async_copy(up_hbm.at[0, half:, :], expert_ref.at[:, hidden : 2 * hidden], sems.at[1]),
+        pltpu.make_async_copy(down_hbm.at[0], expert_ref.at[:, 2 * hidden :], sems.at[2]),
+        pltpu.make_async_copy(w_hbm, w_ref, sems.at[3]),
+        pltpu.make_async_copy(cache_hbm, cache_ref, sems.at[4]),
+    ]
+    for copy in copies:
+        copy.start()
     total = rows * steps
-    local = iota((rows, 1), 0)
-    first = local - local % BEAMS
+    first = iota((rows, 1), 0) // BEAMS * BEAMS
+    diagonal = iota((rows, rows), 0) == iota((rows, rows), 1)
+    eye = diagonal.astype(F32)
+
+    def column(row):
+        return jnp.sum(jnp.where(iota((row.shape[1], row.shape[1]), 0) == iota((row.shape[1], row.shape[1]), 1), row, 0.0), axis=1, keepdims=True)
+
     parent = [
-        (iota((rows, rows), 1) == first + parents_ref[t * rows : (t + 1) * rows, :]).astype(F32).astype(BF16)
+        (iota((rows, rows), 1) == first + column(parents_ref[t : t + 1, :].astype(F32)).astype(jnp.int32)).astype(F32).astype(BF16)
         for t in range(steps)
     ]
-    eye = (iota((rows, rows), 0) == iota((rows, rows), 1)).astype(F32)
     none = jnp.zeros((rows, rows), F32)
     origin = []
     seen = []
@@ -70,29 +90,29 @@
 
     a, b = iota((total, total), 0), iota((total, total), 1)
     same = a // rows == b // rows
-    before = (same & (b < a)).astype(F32).astype(BF16)
     after = (same & (a < b)).astype(F32).astype(BF16)
-    named = [(iota((total, experts), 1) == route_col_ref[:, k : k + 1]).astype(F32) for k in range(2)]
-    count = dot(before, (named[0] + named[1]).astype(BF16))
-    step_at = (iota((total, 1), 0) // rows) * CAP
+    places = [
+        jnp.concatenate([(route_ref[t, k : k + 1, :] + (experts - first_expert)) % experts for t in range(steps)], axis=1)
+        for k in range(2)
+    ]
+    gates = [jnp.concatenate([gate_ref[t, k : k + 1, :] for t in range(steps)], axis=1) for k in range(2)]
+    named = [(iota((experts, total), 0) == places[k]).astype(F32) for k in range(2)]
+    count = dot((named[0] + named[1]).astype(BF16), after)
+    step_at = (iota((1, total), 1) // rows) * CAP
+    chosen = jnp.zeros((experts * PAD, total), F32)
     weights = jnp.zeros((total, experts * PAD), F32)
     for k in range(2):
-        order = jnp.sum(named[k] * count, axis=1, keepdims=True).astype(jnp.int32)
-        target = route_col_ref[:, k : k + 1] * PAD + step_at + order
-        weights += jnp.where(iota((total, experts * PAD), 1) == target, gate_ref[:, k : k + 1], 0.0)
+        order = jnp.sum(named[k] * count, axis=0, keepdims=True).astype(jnp.int32)
+        target = places[k] * PAD + step_at + order
+        chosen += (iota((experts * PAD, total), 0) == target).astype(F32)
+        at = column(target.astype(F32)).astype(jnp.int32)
+        weights += jnp.where(iota((total, experts * PAD), 1) == at, column(gates[k]), 0.0)
+    pack_ref[...] = chosen.astype(BF16)
     high = weights.astype(BF16)
     high_ref[...] = high
     low_ref[...] = (weights - high.astype(F32)).astype(BF16)
-
-    named = [(iota((experts, total), 0) == route_row_ref[k : k + 1, :]).astype(F32) for k in range(2)]
-    count = dot((named[0] + named[1]).astype(BF16), after)
-    step_at = (iota((1, total), 1) // rows) * CAP
-    chosen = jnp.zeros((experts * PAD, total), F32)
-    for k in range(2):
-        order = jnp.sum(named[k] * count, axis=0, keepdims=True).astype(jnp.int32)
-        target = route_row_ref[k : k + 1, :] * PAD + step_at + order
-        chosen += (iota((experts * PAD, total), 0) == target).astype(F32)
-    pack_ref[...] = chosen.astype(BF16)
+    for copy in copies:
+        copy.wait()
 
 
 def normed_blocks(blocks):
@@ -134,17 +154,23 @@
             out_ref[i, g * group * used : (g + 1) * group * used, :] = block
 
 
-def expert_kernel(slots_ref, up_ref, up_other_ref, down_ref, down_other_ref, out_ref):
+def expert_kernel(slots_ref, own_ref, other_ref, out_ref, normed_ref, hidden_ref):
     parts, slots, shard = slots_ref.shape
+    half = own_ref.shape[0]
+    units = half
     block = slots // 3
     for g in range(slots // block):
         at = slice(g * block, (g + 1) * block)
-        normed = normed_blocks([slots_ref[i, at, :].astype(F32) for i in range(parts)])
-        hidden = jax.nn.relu(dot(normed, up_ref[0])).astype(BF16)
-        hidden_other = jax.nn.relu(dot(normed, up_other_ref[0])).astype(BF16)
-        piece = dot(hidden, down_ref[0]) + dot(hidden_other, down_other_ref[0])
-        for i in range(parts):
-            out_ref[i, at, :] = piece[:, i * shard : (i + 1) * shard].astype(BF16)
+        normed_ref[at, :] = normed_blocks([slots_ref[i, at, :].astype(F32) for i in range(parts)])
+    wide = 256
+    for j, ref in enumerate((own_ref, other_ref)):
+        for n in range(0, units, wide):
+            up = dot(normed_ref[:, :half], ref[:, n : n + wide]) + dot(normed_ref[:, half:], ref[:, units + n : units + n + wide])
+            hidden_ref[:, j * units + n : j * units + n + wide] = jax.nn.relu(up).astype(BF16)
+    for i in range(parts):
+        at = slice(2 * units + i * shard, 2 * units + (i + 1) * shard)
+        piece = dot(hidden_ref[:, :units], own_ref[:, at]) + dot(hidden_ref[:, units:], other_ref[:, at])
+        out_ref[i] = piece.astype(BF16)
 
 
 def sum_kernel(used, parts_ref, out_ref):
@@ -172,35 +198,46 @@
     slots = experts * used
     shape = jax.ShapeDtypeStruct
 
+    first_expert = experts // 2 + 4
+    order = [[(p + first_expert) % experts for p in range(experts)]]
+
     def exchange(values, axis):
-        return lax.all_to_all(values, axis, split_axis=0, concat_axis=0, tiled=True)
+        groups = order if axis == "yz" else None
+        return lax.all_to_all(values, axis, split_axis=0, concat_axis=0, tiled=True, axis_index_groups=groups)
 
     tokens = embeds.reshape(total, shard)
     gathered = exchange(jnp.broadcast_to(tokens[None], (parts, total, shard)), "x")
-    swap = [(i, (i + 1) % CORES) for i in range(CORES)]
-    up_other = lax.ppermute(w_up, "core", swap)
-    down_other = lax.ppermute(w_down, "core", swap)
-    bias, pack, high, low = call(
-        functools.partial(plan_kernel, rows, steps, prefix, experts),
+    half, hidden = width // 2, w_up.shape[2]
+    bias, pack, high, low, w_here, cache_here, own = call(
+        functools.partial(plan_kernel, rows, steps, prefix, experts, first_expert),
         (
             shape((total, rows * prefix + HD), F32),
             shape((experts * PAD, total), BF16),
             shape((total, experts * PAD), BF16),
             shape((total, experts * PAD), BF16),
+            shape((3, width, shard), BF16),
+            shape(prefix_cache.shape, BF16),
+            shape((half, 2 * hidden + width), BF16),
         ),
-        parents.reshape(total, 1),
-        routes.transpose(2, 0, 1).reshape(2, total),
-        routes.reshape(total, 2),
-        gates.reshape(total, 2),
-        cost=(10**8, 10**6),
-    )
+        parents,
+        routes.transpose(0, 2, 1),
+        gates.transpose(0, 2, 1),
+        w_qkv.transpose(1, 0, 2),
+        prefix_cache,
+        w_up,
+        w_down,
+        cost=(10**8, 5 * 10**6),
+        in_hbm=(3, 4, 5, 6),
+        scratch=[pltpu.SemaphoreType.DMA((5,))],
+    )
+    other = lax.ppermute(own, "core", [(i, (i + 1) % CORES) for i in range(CORES)])
     middle, packed = call(
         functools.partial(attend_kernel, prefix),
         (shape((total, shard), BF16), shape((experts * PAD, shard), BF16)),
         gathered,
         tokens,
-        w_qkv.transpose(1, 0, 2),
-        prefix_cache,
+        w_here,
+        cache_here,
         bias,
         pack,
         cost=(2 * total * width * 3 * shard, 3 * 10**6),
@@ -212,11 +249,10 @@
         expert_kernel,
         shape((parts, slots, shard), BF16),
         whole,
-        w_up,
-        up_other,
-        w_down,
-        down_other,
-        cost=(8 * slots * width * w_up.shape[2], 6 * 10**6),
+        own,
+        other,
+        cost=(8 * slots * width * hidden, 6 * 10**6),
+        scratch=[pltpu.VMEM((slots, width), BF16), pltpu.VMEM((slots, 2 * hidden), BF16)],
     )
     pieces = exchange(share, "x")
     summed = call(functools.partial(sum_kernel, used), shape((experts * PAD, shard), BF16), pieces)

time: 99.6 us -> 96.6 us (0.970)
  the two profiles are of different devices: /device:TPU:2 before, /device:TPU:8 now
where the time goes in v2:
time: 96.6 us; the launch traced here: 96.1 us
  blocking collectives  80.9 us (84%)
  local copies, waits for them, and re-layouts  7.14 us (7%)
  Pallas kernels  6.04 us (6%)
  starting transfers between devices  1.92 us (2%)
    all_to_all x5, blocking collectives, exchange(): lax.all_to_all(values, axis, split_axis=0, concat_axis=0, tiled=True, axi...  80.9 us
    unnamed x16, local copies, waits for them, and re-layouts  7.13 us
    pallas_call x6, Pallas kernels, call(): pl.pallas_call(kernel, out_shape=outs, in_specs=[pl.BlockSpec(memory_spac...  6.04 us
  transfers between devices with their start and end apart: 1, of which 0 were waited for; matrix products, arithmetic and copies ran while one was open for 0% of the time, Pallas kernels for 1%

profile of v2, /device:TPU:8, one launch (start us, length us, event | category | flops | bytes accessed | tf_op | source)
XLA Modules:
  0.0 96.1 jit_solution(14061684301013202471)
XLA Ops:
  0.0 0.0 copy-start
  0.0 1.4 %copy-done = bf16[1024,3,256]{2,0,1:T(8,128)(2,1)S(1)} copy-done((bf16[1024,3,256]{2,0,1:T(8,128)(2,1)S(1)}, bf16[1024,3,256]{2,0,1:T(8,128)(2,1)}, u32[]{:S(2)}) %copy-start) | copy-done | bytes 1572888
  1.4 0.0 copy-start.1
  1.4 1.2 %copy-done.1 = bf16[16,2,64,256]{3,2,1,0:T(8,128)(2,1)S(1)} copy-done((bf16[16,2,64,256]{3,2,1,0:T(8,128)(2,1)S(1)}, bf16[16,2,64,256]{3,2,1,0:T(8,128)(2,1)}, u32[]{:S(2)}) %copy-start.1) | copy-done | bytes 1048600
  2.6 0.0 copy-start.2
  2.6 1.2 %copy-done.2 = bf16[1,1024,512]{2,1,0:T(8,128)(2,1)S(1)} copy-done((bf16[1,1024,512]{2,1,0:T(8,128)(2,1)S(1)}, bf16[1,1024,512]{2,1,0:T(8,128)(2,1)}, u32[]{:S(2)}) %copy-start.2) | copy-done | bytes 1048600
  3.9 0.0 copy-start.3
  3.9 1.2 %copy-done.3 = bf16[1,512,1024]{2,1,0:T(8,128)(2,1)S(1)} copy-done((bf16[1,512,1024]{2,1,0:T(8,128)(2,1)S(1)}, bf16[1,512,1024]{2,1,0:T(8,128)(2,1)}, u32[]{:S(2)}) %copy-start.3) | copy-done | bytes 1048600
  5.1 0.0 copy-start.5
  5.1 0.7 copy-done.5
  5.8 0.0 copy-start.6
  5.8 0.7 copy-done.6
  6.5 0.0 copy-start.7
  6.5 0.7 copy-done.7
  7.1 0.0 copy-start.4
  7.1 1.3 %shard_map.82 = (f32[48,1152]{1,0:T(8,128)S(1)}, bf16[512,48]{1,0:T(8,128)(2,1)S(1)}, bf16[48,512]{1,0:T(8,128)(2,1)S(1)}, bf16[48,512]{1,0:T(8,128)(2,1)S(1)}, ...) custom-call(s32[3,16]{1,0:T(4,128)S(1)} %copy-done.7, ...), custom_call_target="tpu_custom_call" | custom-call | flops 100000000 | bytes 5000000 | tf_op jit(solution)/shard_map/pallas_call | solution.py:35
  8.4 1.9 %collective-permute-start = (bf16[512,2048]{1,0:T(8,128)(2,1)S(1)}, bf16[512,2048]{1,0:T(8,128)(2,1)S(1)}, u32[]{:S(2)}, u32[]{:S(2)}) collective-permute-start(bf16[512,2048]{1,0:T(8,128)(2,1)S(1)} %get-tuple-element.20.own_ref), channel_id=1, source_target_pairs={{0,1},{1,0},{2,3},{3,2},{4,5},{5,4},{6,7},{7,6},{8,9},{9,8},{10,11... | collective-permute-start | bytes 6291464 | tf_op jit(solution)/shard_map/ppermute | solution.py:233
  10.4 0.0 copy-done.4
  10.4 9.9 %all_to_all.25.gathered_ref = bf16[4,48,256]{2,1,0:T(8,128)(2,1)S(1)} all-to-all(bf16[4,48,256]{2,1,0:T(8,128)(2,1)S(1)} %broadcast_in_dim.8), channel_id=1, replica_groups=mesh['x'=4,'yz'=64,'core'=2] {'x'}, dimensions={0} | all-to-all | bytes 196608 | tf_op jit(solution)/shard_map/all_to_all | solution.py:206
  20.3 1.2 %shard_map.83 = (bf16[48,256]{1,0:T(8,128)(2,1)S(1)}, bf16[512,256]{1,0:T(8,128)(2,1)S(1)}) custom-call(bf16[4,48,256]{2,1,0:T(8,128)(2,1)S(1)} %all_to_all.25.gathered_ref, bf16[48,256]{1,0:T(8,128)(2,1)S(1)} %bitcast.15, bf16[3,1024,256]{2,1,0:T(8,128)(2,1)S(1)} %get-tuple-element.14.w_ref, bf16[16,2,64,256]{3,2,1,0:T(8,128)(2,1)S(1)} %get-tuple-element.15.cache_ref, ...), custom_call_target="tpu_custom_call" | custom-call | flops 75497472 | bytes 3000000 | tf_op jit(solution)/shard_map/pallas_call | solution.py:35
  21.5 24.9 %all_to_all.26 = bf16[64,8,256]{2,1,0:T(8,128)(2,1)S(1)} all-to-all(bf16[64,8,256]{2,1,0:T(8,128)(2,1)S(1)} %bitcast.13), channel_id=1, replica_groups={{72,74,76,78,80,82,84,86,88,90,92,94,96,98,100,102,104,106,108,110,112,..., dimensions={0} | all-to-all | bytes 524288 | tf_op jit(solution)/shard_map/all_to_all | solution.py:206
  46.4 0.2 shard_map.84
  46.6 14.2 %all_to_all.27.slots_ref = bf16[4,384,256]{2,1,0:T(8,128)(2,1)S(1)} all-to-all(bf16[4,384,256]{2,1,0:T(8,128)(2,1)S(1)} %shard_map.84), channel_id=1, replica_groups=mesh['x'=4,'yz'=64,'core'=2] {'x'}, dimensions={0} | all-to-all | bytes 1572864 | tf_op jit(solution)/shard_map/all_to_all | solution.py:206
  60.8 0.0 collective-permute-done.other_ref
  60.8 2.3 %shard_map.85 = bf16[4,384,256]{2,1,0:T(8,128)(2,1)S(1)} custom-call(bf16[4,384,256]{2,1,0:T(8,128)(2,1)S(1)} %all_to_all.27.slots_ref, bf16[512,2048]{1,0:T(8,128)(2,1)S(1)} %get-tuple-element.20.own_ref, bf16[512,2048]{1,0:T(8,128)(2,1)S(1)} %collective-permute-done.other_ref), custom_call_target="tpu_custom_call" | custom-call | flops 1610612736 | bytes 6000000 | tf_op jit(solution)/shard_map/pallas_call | solution.py:35
  63.1 13.0 %all_to_all.28.parts_ref = bf16[4,384,256]{2,1,0:T(8,128)(2,1)S(1)} all-to-all(bf16[4,384,256]{2,1,0:T(8,128)(2,1)S(1)} %shard_map.85), channel_id=1, replica_groups=mesh['x'=4,'yz'=64,'core'=2] {'x'}, dimensions={0} | all-to-all | bytes 1572864 | tf_op jit(solution)/shard_map/all_to_all | solution.py:206
  76.1 0.3 shard_map.86
  76.4 19.0 %all_to_all.29 = bf16[64,8,256]{2,1,0:T(8,128)(2,1)S(1)} all-to-all(bf16[64,8,256]{2,1,0:T(8,128)(2,1)S(1)} %bitcast.12), channel_id=1, replica_groups={{72,74,76,78,80,82,84,86,88,90,92,94,96,98,100,102,104,106,108,110,112,..., dimensions={0} | all-to-all | bytes 524288 | tf_op jit(solution)/shard_map/all_to_all | solution.py:206
  95.3 0.8 shard_map.87
  (1 shorter events, 0.0 us)
Async XLA Ops:
  0.0 1.4 %copy-start = (bf16[1024,3,256]{2,0,1:T(8,128)(2,1)S(1)}, bf16[1024,3,256]{2,0,1:T(8,128)(2,1)}, u32[]{:S(2)}) copy-start(bf16[1024,3,256]{2,0,1:T(8,128)(2,1)} %param.10) | copy-start | bytes 4718596
  1.4 1.2 %copy-start.1 = (bf16[16,2,64,256]{3,2,1,0:T(8,128)(2,1)S(1)}, bf16[16,2,64,256]{3,2,1,0:T(8,128)(2,1)}, u32[]{:S(2)}) copy-start(bf16[16,2,64,256]{3,2,1,0:T(8,128)(2,1)} %cache_hbm.1) | copy-start | bytes 3145732
  2.6 1.2 %copy-start.2 = (bf16[1,1024,512]{2,1,0:T(8,128)(2,1)S(1)}, bf16[1,1024,512]{2,1,0:T(8,128)(2,1)}, u32[]{:S(2)}) copy-start(bf16[1,1024,512]{2,1,0:T(8,128)(2,1)} %up_hbm.1) | copy-start | bytes 3145732
  3.9 1.2 %copy-start.3 = (bf16[1,512,1024]{2,1,0:T(8,128)(2,1)S(1)}, bf16[1,512,1024]{2,1,0:T(8,128)(2,1)}, u32[]{:S(2)}) copy-start(bf16[1,512,1024]{2,1,0:T(8,128)(2,1)} %down_hbm.1) | copy-start | bytes 3145732
  5.1 0.7 copy-start.5
  5.8 0.7 copy-start.6
  6.5 0.7 copy-start.7
  7.1 3.2 %copy-start.4 = (bf16[3,16,256]{2,1,0:T(8,128)(2,1)S(1)}, bf16[3,16,256]{2,1,0:T(8,128)(2,1)}, u32[]{:S(2)}) copy-start(bf16[3,16,256]{2,1,0:T(8,128)(2,1)} %param.8) | copy-start | bytes 73732
  8.4 52.4 %collective-permute-start = (bf16[512,2048]{1,0:T(8,128)(2,1)S(1)}, bf16[512,2048]{1,0:T(8,128)(2,1)S(1)}, u32[]{:S(2)}, u32[]{:S(2)}) collective-permute-start(bf16[512,2048]{1,0:T(8,128)(2,1)S(1)} %get-tuple-element.20.own_ref), channel_id=1, source_target_pairs={{0,1},{1,0},{2,3},{3,2},{4,5},{5,4},{6,7},{7,6},{8,9},{9,8},{10,11... | collective-permute-start | bytes 6291464 | tf_op jit(solution)/shard_map/ppermute | solution.py:233

commit v3 on v2

--- a/solution.py
+++ b/solution.py
@@ -30,35 +30,28 @@
     return lax.dot_general(a, b, (((1,), (1,)), ((), ())), preferred_element_type=F32)
 
 
-def call(kernel, outs, *args, cost=None, in_hbm=(), scratch=()):
+def call(kernel, outs, *args, cost=None, in_hbm=(), out_hbm=(), scratch=(), limit=16):
     flops, nbytes = cost or (0, 0)
     return pl.pallas_call(
         kernel,
         out_shape=outs,
-        in_specs=[pl.BlockSpec(memory_space=pl.ANY if i in in_hbm else pltpu.VMEM) for i in range(len(args))],
-        out_specs=jax.tree.map(lambda _: pl.BlockSpec(memory_space=pltpu.VMEM), outs),
+        in_specs=[pl.BlockSpec(memory_space=pltpu.HBM if i in in_hbm else pltpu.VMEM) for i in range(len(args))],
+        out_specs=[pl.BlockSpec(memory_space=pltpu.HBM if i in out_hbm else pltpu.VMEM) for i in range(len(outs))],
         scratch_shapes=scratch,
-        compiler_params=pltpu.CompilerParams(vmem_limit_bytes=16 * 1024 * 1024),
+        compiler_params=pltpu.CompilerParams(vmem_limit_bytes=limit * 1024 * 1024),
         cost_estimate=pl.CostEstimate(flops=flops, bytes_accessed=nbytes, transcendentals=0),
     )(*args)
 
 
+def copies_kernel(token_ref, out_ref):
+    for i in range(out_ref.shape[0]):
+        out_ref[i] = token_ref[...]
+
+
 def plan_kernel(
     rows, steps, prefix, experts, first_expert,
-    parents_ref, route_ref, gate_ref, w_hbm, cache_hbm, up_hbm, down_hbm,
-    bias_ref, pack_ref, high_ref, low_ref, w_ref, cache_ref, expert_ref, sems,
+    parents_ref, route_ref, gate_ref, bias_ref, pack_ref, high_ref, low_ref,
 ):
-    half = up_hbm.shape[1] // 2
-    hidden = up_hbm.shape[2]
-    copies = [
-        pltpu.make_async_copy(up_hbm.at[0, :half, :], expert_ref.at[:, :hidden], sems.at[0]),
-        pltpu.make_async_copy(up_hbm.at[0, half:, :], expert_ref.at[:, hidden : 2 * hidden], sems.at[1]),
-        pltpu.make_async_copy(down_hbm.at[0], expert_ref.at[:, 2 * hidden :], sems.at[2]),
-        pltpu.make_async_copy(w_hbm, w_ref, sems.at[3]),
-        pltpu.make_async_copy(cache_hbm, cache_ref, sems.at[4]),
-    ]
-    for copy in copies:
-        copy.start()
     total = rows * steps
     first = iota((rows, 1), 0) // BEAMS * BEAMS
     diagonal = iota((rows, rows), 0) == iota((rows, rows), 1)
@@ -111,8 +104,6 @@
     high = weights.astype(BF16)
     high_ref[...] = high
     low_ref[...] = (weights - high.astype(F32)).astype(BF16)
-    for copy in copies:
-        copy.wait()
 
 
 def normed_blocks(blocks):
@@ -154,23 +145,42 @@
             out_ref[i, g * group * used : (g + 1) * group * used, :] = block
 
 
-def expert_kernel(slots_ref, own_ref, other_ref, out_ref, normed_ref, hidden_ref):
+def expert_kernel(
+    slots_ref, up_ref, down_ref, up_other_hbm, down_other_hbm,
+    out_ref, normed_ref, hidden_ref, sum_ref, up_other_ref, down_other_ref, sems,
+):
     parts, slots, shard = slots_ref.shape
-    half = own_ref.shape[0]
-    units = half
+    width, units = up_ref.shape[1:]
+    copies = []
+    for source, target in ((up_other_hbm, up_other_ref), (down_other_hbm, down_other_ref)):
+        rows = source.shape[1] // 4
+        for g in range(4):
+            at = (0, slice(g * rows, (g + 1) * rows))
+            copies.append(pltpu.make_async_copy(source.at[at], target.at[at], sems.at[len(copies)]))
+    for copy in copies:
+        copy.start()
     block = slots // 3
     for g in range(slots // block):
         at = slice(g * block, (g + 1) * block)
         normed_ref[at, :] = normed_blocks([slots_ref[i, at, :].astype(F32) for i in range(parts)])
     wide = 256
-    for j, ref in enumerate((own_ref, other_ref)):
+
+    def hide(ref):
         for n in range(0, units, wide):
-            up = dot(normed_ref[:, :half], ref[:, n : n + wide]) + dot(normed_ref[:, half:], ref[:, units + n : units + n + wide])
-            hidden_ref[:, j * units + n : j * units + n + wide] = jax.nn.relu(up).astype(BF16)
+            hidden_ref[:, n : n + wide] = jax.nn.relu(dot(normed_ref[...], ref[0, :, n : n + wide])).astype(BF16)
+
+    hide(up_ref)
     for i in range(parts):
-        at = slice(2 * units + i * shard, 2 * units + (i + 1) * shard)
-        piece = dot(hidden_ref[:, :units], own_ref[:, at]) + dot(hidden_ref[:, units:], other_ref[:, at])
-        out_ref[i] = piece.astype(BF16)
+        at = slice(i * shard, (i + 1) * shard)
+        sum_ref[:, at] = dot(hidden_ref[...], down_ref[0, :, at])
+    for copy in copies[:4]:
+        copy.wait()
+    hide(up_other_ref)
+    for copy in copies[4:]:
+        copy.wait()
+    for i in range(parts):
+        at = slice(i * shard, (i + 1) * shard)
+        out_ref[i] = (sum_ref[:, at] + dot(hidden_ref[...], down_other_ref[0, :, at])).astype(BF16)
 
 
 def sum_kernel(used, parts_ref, out_ref):
@@ -206,58 +216,63 @@
         return lax.all_to_all(values, axis, split_axis=0, concat_axis=0, tiled=True, axis_index_groups=groups)
 
     tokens = embeds.reshape(total, shard)
-    gathered = exchange(jnp.broadcast_to(tokens[None], (parts, total, shard)), "x")
-    half, hidden = width // 2, w_up.shape[2]
-    bias, pack, high, low, w_here, cache_here, own = call(
+    (copies,) = call(copies_kernel, [shape((parts, total, shard), BF16)], tokens, cost=(10**9, 10**7))
+    gathered = exchange(copies, "x")
+    hidden = w_up.shape[2]
+    swap = [(i, (i + 1) % CORES) for i in range(CORES)]
+    up_other = lax.ppermute(w_up, "core", swap)
+    down_other = lax.ppermute(w_down, "core", swap)
+    bias, pack, high, low = call(
         functools.partial(plan_kernel, rows, steps, prefix, experts, first_expert),
         (
             shape((total, rows * prefix + HD), F32),
             shape((experts * PAD, total), BF16),
             shape((total, experts * PAD), BF16),
             shape((total, experts * PAD), BF16),
-            shape((3, width, shard), BF16),
-            shape(prefix_cache.shape, BF16),
-            shape((half, 2 * hidden + width), BF16),
         ),
         parents,
         routes.transpose(0, 2, 1),
         gates.transpose(0, 2, 1),
-        w_qkv.transpose(1, 0, 2),
-        prefix_cache,
-        w_up,
-        w_down,
-        cost=(10**8, 5 * 10**6),
-        in_hbm=(3, 4, 5, 6),
-        scratch=[pltpu.SemaphoreType.DMA((5,))],
-    )
-    other = lax.ppermute(own, "core", [(i, (i + 1) % CORES) for i in range(CORES)])
+        cost=(10**9, 10**7),
+    )
+    gathered, up_other, down_other = lax.optimization_barrier((gathered, up_other, down_other))
     middle, packed = call(
         functools.partial(attend_kernel, prefix),
         (shape((total, shard), BF16), shape((experts * PAD, shard), BF16)),
         gathered,
         tokens,
-        w_here,
-        cache_here,
+        w_qkv.transpose(1, 0, 2),
+        prefix_cache,
         bias,
         pack,
         cost=(2 * total * width * 3 * shard, 3 * 10**6),
     )
     arrived = exchange(packed.reshape(experts, PAD, shard), "yz").reshape(experts * PAD, shard)
-    spread = call(functools.partial(spread_kernel, used), shape((parts, slots, shard), BF16), arrived)
+    (spread,) = call(functools.partial(spread_kernel, used), [shape((parts, slots, shard), BF16)], arrived)
     whole = exchange(spread, "x")
-    share = call(
+    (share,) = call(
         expert_kernel,
-        shape((parts, slots, shard), BF16),
+        [shape((parts, slots, shard), BF16)],
         whole,
-        own,
-        other,
+        w_up,
+        w_down,
+        up_other,
+        down_other,
         cost=(8 * slots * width * hidden, 6 * 10**6),
-        scratch=[pltpu.VMEM((slots, width), BF16), pltpu.VMEM((slots, 2 * hidden), BF16)],
+        in_hbm=(3, 4),
+        scratch=[
+            pltpu.VMEM((slots, width), BF16),
+            pltpu.VMEM((slots, hidden), BF16),
+            pltpu.VMEM((slots, width), F32),
+            pltpu.VMEM(w_up.shape, BF16),
+            pltpu.VMEM(w_down.shape, BF16),
+            pltpu.SemaphoreType.DMA((8,)),
+        ],
     )
     pieces = exchange(share, "x")
-    summed = call(functools.partial(sum_kernel, used), shape((experts * PAD, shard), BF16), pieces)
+    (summed,) = call(functools.partial(sum_kernel, used), [shape((experts * PAD, shard), BF16)], pieces)
     returned = exchange(summed.reshape(experts, PAD, shard), "yz").reshape(experts * PAD, shard)
-    mixed = call(combine_kernel, shape((total, shard), BF16), middle, returned, high, low)
+    (mixed,) = call(combine_kernel, [shape((total, shard), BF16)], middle, returned, high, low)
     return mixed.reshape(steps, rows, shard)
 
 

time: 96.6 us -> 89.7 us (0.929)
  blocking collectives: 80.9 us -> 67.2 us
  starting transfers between devices: 1.92 us -> 8.61 us
  local copies, waits for them, and re-layouts: 7.14 us -> 0.78 us
  waiting for transfers between devices: 0.01 us -> 5.04 us
  Pallas kernels: 6.04 us -> 7.39 us
    all_to_all x5 -> x4, blocking collectives: 80.9 us -> 67.2 us  [exchange(): lax.all_to_all(values, axis, split_axis=0, concat_axis=0, tiled=True, axi...]
    unnamed x16 -> x18, local copies, waits for them, and re-layouts: 7.13 us -> 0.78 us
    all_to_all x0 -> x1, waiting for transfers between devices: none -> 5.03 us  [exchange(): lax.all_to_all(values, axis, split_axis=0, concat_axis=0, tiled=True, axi...]
    all_to_all x0 -> x1, starting transfers between devices: none -> 4.29 us  [exchange(): lax.all_to_all(values, axis, split_axis=0, concat_axis=0, tiled=True, axi...]
    ppermute x1 -> x2, starting transfers between devices: 1.92 us -> 4.32 us  [the longest x1 2.41 us: shards(): down_other = lax.ppermute(w_down, 'core', swap)]
    pallas_call x6 -> x7, Pallas kernels: 6.04 us -> 7.39 us  [call(): pl.pallas_call(kernel, out_shape=outs, in_specs=[pl.BlockSpec(memory_spac...]
  transfers between devices with their start and end apart: 1 -> 3, of which waited for: 0 -> 1; matrix products, arithmetic and copies ran while one was open for 0% -> 0% of each run, Pallas kernels for 1% -> 2%
where the time goes in v3:
time: 89.7 us; the launch traced here: 89.2 us
  blocking collectives  67.2 us (75%)
  starting transfers between devices  8.61 us (10%)
  Pallas kernels  7.39 us (8%)
  waiting for transfers between devices  5.04 us (6%)
    all_to_all x4, blocking collectives, exchange(): lax.all_to_all(values, axis, split_axis=0, concat_axis=0, tiled=True, axi...  67.2 us
    pallas_call x7, Pallas kernels, call(): pl.pallas_call(kernel, out_shape=outs, in_specs=[pl.BlockSpec(memory_spac...  7.39 us
    all_to_all x1, waiting for transfers between devices, exchange(): lax.all_to_all(values, axis, split_axis=0, concat_axis=0, tiled=True, axi...  5.03 us
    all_to_all x1, starting transfers between devices, exchange(): lax.all_to_all(values, axis, split_axis=0, concat_axis=0, tiled=True, axi...  4.29 us
    ppermute x1, starting transfers between devices, shards(): down_other = lax.ppermute(w_down, 'core', swap)  2.41 us
    ppermute x1, starting transfers between devices, shards(): up_other = lax.ppermute(w_up, 'core', swap)  1.91 us
  transfers between devices with their start and end apart: 3, of which 1 were waited for; matrix products, arithmetic and copies ran while one was open for 0% of the time, Pallas kernels for 2%

profile of v3, /device:TPU:8, one launch (start us, length us, event | category | flops | bytes accessed | tf_op | source)
XLA Modules:
  0.0 89.2 jit_solution(13136078276645332386)
XLA Ops:
  0.0 1.9 %collective-permute-start = (bf16[1,1024,512]{2,1,0:T(8,128)(2,1)}, bf16[1,1024,512]{2,1,0:T(8,128)(2,1)}, u32[]{:S(2)}, u32[]{:S(2)}) collective-permute-start(bf16[1,1024,512]{2,1,0:T(8,128)(2,1)} %up_ref.1), channel_id=1, source_target_pairs={{0,1},{1,0},{2,3},{3,2},{4,5},{5,4},{6,7},{7,6},{8,9},{9,8},{10,11... | collective-permute-start | bytes 3145736 | tf_op jit(solution)/shard_map/ppermute | solution.py:223
  1.9 2.4 %collective-permute-start.1 = (bf16[1,512,1024]{2,1,0:T(8,128)(2,1)}, bf16[1,512,1024]{2,1,0:T(8,128)(2,1)}, u32[]{:S(2)}, u32[]{:S(2)}) collective-permute-start(bf16[1,512,1024]{2,1,0:T(8,128)(2,1)} %down_ref.1), channel_id=1, source_target_pairs={{0,1},{1,0},{2,3},{3,2},{4,5},{5,4},{6,7},{7,6},{8,9},{9,8},{10,11... | collective-permute-start | bytes 3145736 | tf_op jit(solution)/shard_map/ppermute | solution.py:224
  4.3 0.0 copy-start.2
  4.3 0.7 copy-done.2
  5.1 0.6 shard_map.82
  5.7 4.3 %all-to-all-start = ((bf16[4,48,256]{2,1,0:T(8,128)(2,1)}), bf16[4,48,256]{2,1,0:T(8,128)(2,1)S(1)}, u32[]{:S(2)}, u32[]{:S(2)}) async-start(bf16[4,48,256]{2,1,0:T(8,128)(2,1)} %shard_map.82), calls=%async_computation | async-start | bytes 196608 | tf_op jit(solution)/shard_map/all_to_all | solution.py:216
  10.0 0.0 copy-done.6
  10.0 0.0 copy-done.7
  10.0 0.0 copy-done.8
  10.0 0.0 copy-start
  10.0 0.0 copy-start.1
  10.1 0.0 copy-start.3
  10.1 0.7 shard_map.83
  10.8 5.0 %all-to-all-done.gathered_ref = bf16[4,48,256]{2,1,0:T(8,128)(2,1)S(1)} async-done(((bf16[4,48,256]{2,1,0:T(8,128)(2,1)}), bf16[4,48,256]{2,1,0:T(8,128)(2,1)S(1)}, u32[]{:S(2)}, u32[]{:S(2)}) %all-to-all-start) | async-done | bytes 98336 | tf_op jit(solution)/shard_map/all_to_all | solution.py:216
  15.8 0.0 collective-permute-done.up_other_hbm
  15.8 0.0 collective-permute-done.1.down_other_hbm
  15.8 0.0 copy-done
  15.8 0.0 copy-done.1
  15.8 0.0 copy-done.3
  15.9 1.2 %shard_map.84 = (bf16[48,256]{1,0:T(8,128)(2,1)S(1)}, bf16[512,256]{1,0:T(8,128)(2,1)S(1)}) custom-call(bf16[4,48,256]{2,1,0:T(8,128)(2,1)S(1)} %all-to-all-done.gathered_ref, bf16[48,256]{1,0:T(8,128)(2,1)S(1)} %bitcast.15, bf16[3,1024,256]{2,1,0:T(8,128)(2,1)S(1)} %bitcast.9, bf16[16,2,64,256]{3,2,1,0:T(8,128)(2,1)S(1)} %copy-done.1, ...), custom_call_target="tpu_custom_call" | custom-call | flops 75497472 | bytes 3000000 | tf_op jit(solution)/shard_map/pallas_call | solution.py:35
  17.1 0.0 copy-start.4
  17.1 0.0 copy-start.5
  17.1 24.5 %all_to_all.25 = bf16[64,8,256]{2,1,0:T(8,128)(2,1)S(1)} all-to-all(bf16[64,8,256]{2,1,0:T(8,128)(2,1)S(1)} %bitcast.13), channel_id=1, replica_groups={{72,74,76,78,80,82,84,86,88,90,92,94,96,98,100,102,104,106,108,110,112,..., dimensions={0} | all-to-all | bytes 524288 | tf_op jit(solution)/shard_map/all_to_all | solution.py:216
  41.6 0.2 shard_map.85
  41.8 13.2 %all_to_all.26.slots_ref = bf16[4,384,256]{2,1,0:T(8,128)(2,1)S(1)} all-to-all(bf16[4,384,256]{2,1,0:T(8,128)(2,1)S(1)} %shard_map.85), channel_id=1, replica_groups=mesh['x'=4,'yz'=64,'core'=2] {'x'}, dimensions={0} | all-to-all | bytes 1572864 | tf_op jit(solution)/shard_map/all_to_all | solution.py:216
  55.0 0.0 copy-done.4
  55.0 0.0 copy-done.5
  55.0 3.5 %shard_map.86 = bf16[4,384,256]{2,1,0:T(8,128)(2,1)S(1)} custom-call(bf16[4,384,256]{2,1,0:T(8,128)(2,1)S(1)} %all_to_all.26.slots_ref, bf16[1,1024,512]{2,1,0:T(8,128)(2,1)S(1)} %copy-done.4, bf16[1,512,1024]{2,1,0:T(8,128)(2,1)S(1)} %copy-done.5, bf16[1,1024,512]{2,1,0:T(8,128)(2,1)} %collective-permute-done.up_other_hbm, ...), custom_call_target="tpu_custom_call" | custom-call | flops 1610612736 | bytes 6000000 | tf_op jit(solution)/shard_map/pallas_call | solution.py:35
  58.6 12.3 %all_to_all.27.parts_ref = bf16[4,384,256]{2,1,0:T(8,128)(2,1)S(1)} all-to-all(bf16[4,384,256]{2,1,0:T(8,128)(2,1)S(1)} %shard_map.86), channel_id=1, replica_groups=mesh['x'=4,'yz'=64,'core'=2] {'x'}, dimensions={0} | all-to-all | bytes 1572864 | tf_op jit(solution)/shard_map/all_to_all | solution.py:216
  70.9 0.3 shard_map.87
  71.1 17.2 %all_to_all.28 = bf16[64,8,256]{2,1,0:T(8,128)(2,1)S(1)} all-to-all(bf16[64,8,256]{2,1,0:T(8,128)(2,1)S(1)} %bitcast.12), channel_id=1, replica_groups={{72,74,76,78,80,82,84,86,88,90,92,94,96,98,100,102,104,106,108,110,112,..., dimensions={0} | all-to-all | bytes 524288 | tf_op jit(solution)/shard_map/all_to_all | solution.py:216
  88.4 0.8 shard_map.88
  (3 shorter events, 0.0 us)
Async XLA Ops:
  0.0 15.8 %collective-permute-start = (bf16[1,1024,512]{2,1,0:T(8,128)(2,1)}, bf16[1,1024,512]{2,1,0:T(8,128)(2,1)}, u32[]{:S(2)}, u32[]{:S(2)}) collective-permute-start(bf16[1,1024,512]{2,1,0:T(8,128)(2,1)} %up_ref.1), channel_id=1, source_target_pairs={{0,1},{1,0},{2,3},{3,2},{4,5},{5,4},{6,7},{7,6},{8,9},{9,8},{10,11... | collective-permute-start | bytes 3145736 | tf_op jit(solution)/shard_map/ppermute | solution.py:223
  1.9 13.9 %collective-permute-start.1 = (bf16[1,512,1024]{2,1,0:T(8,128)(2,1)}, bf16[1,512,1024]{2,1,0:T(8,128)(2,1)}, u32[]{:S(2)}, u32[]{:S(2)}) collective-permute-start(bf16[1,512,1024]{2,1,0:T(8,128)(2,1)} %down_ref.1), channel_id=1, source_target_pairs={{0,1},{1,0},{2,3},{3,2},{4,5},{5,4},{6,7},{7,6},{8,9},{9,8},{10,11... | collective-permute-start | bytes 3145736 | tf_op jit(solution)/shard_map/ppermute | solution.py:224
  4.3 0.7 copy-start.2
  5.1 4.9 %copy-start.6 = (s32[3,16,2]{1,2,0:T(2,128)S(1)}, s32[3,16,2]{1,2,0:T(2,128)}, u32[]{:S(2)}) copy-start(s32[3,16,2]{1,2,0:T(2,128)} %param.14) | copy-start | bytes 1156
  5.1 4.9 %copy-start.7 = (f32[3,16,2]{1,2,0:T(2,128)S(1)}, f32[3,16,2]{1,2,0:T(2,128)}, u32[]{:S(2)}) copy-start(f32[3,16,2]{1,2,0:T(2,128)} %param.15) | copy-start | bytes 1156
  5.1 4.9 %copy-start.8 = (s32[3,16]{1,0:T(4,128)S(1)}, s32[3,16]{1,0:T(4,128)}, u32[]{:S(2)}) copy-start(s32[3,16]{1,0:T(4,128)} %parents_ref.1) | copy-start | bytes 580
  5.7 10.1 %all-to-all-start = ((bf16[4,48,256]{2,1,0:T(8,128)(2,1)}), bf16[4,48,256]{2,1,0:T(8,128)(2,1)S(1)}, u32[]{:S(2)}, u32[]{:S(2)}) async-start(bf16[4,48,256]{2,1,0:T(8,128)(2,1)} %shard_map.82), calls=%async_computation | async-start | bytes 196608 | tf_op jit(solution)/shard_map/all_to_all | solution.py:216
  10.0 5.8 %copy-start = (bf16[1024,3,256]{2,0,1:T(8,128)(2,1)S(1)}, bf16[1024,3,256]{2,0,1:T(8,128)(2,1)}, u32[]{:S(2)}) copy-start(bf16[1024,3,256]{2,0,1:T(8,128)(2,1)} %param.10) | copy-start | bytes 4718596
  10.0 5.8 %copy-start.1 = (bf16[16,2,64,256]{3,2,1,0:T(8,128)(2,1)S(1)}, bf16[16,2,64,256]{3,2,1,0:T(8,128)(2,1)}, u32[]{:S(2)}) copy-start(bf16[16,2,64,256]{3,2,1,0:T(8,128)(2,1)} %cache_ref.1) | copy-start | bytes 3145732
  10.1 5.8 %copy-start.3 = (bf16[3,16,256]{2,1,0:T(8,128)(2,1)S(1)}, bf16[3,16,256]{2,1,0:T(8,128)(2,1)}, u32[]{:S(2)}) copy-start(bf16[3,16,256]{2,1,0:T(8,128)(2,1)} %param.8) | copy-start | bytes 73732
  17.1 37.9 %copy-start.4 = (bf16[1,1024,512]{2,1,0:T(8,128)(2,1)S(1)}, bf16[1,1024,512]{2,1,0:T(8,128)(2,1)}, u32[]{:S(2)}) copy-start(bf16[1,1024,512]{2,1,0:T(8,128)(2,1)} %up_ref.1) | copy-start | bytes 3145732
  17.1 37.9 %copy-start.5 = (bf16[1,512,1024]{2,1,0:T(8,128)(2,1)S(1)}, bf16[1,512,1024]{2,1,0:T(8,128)(2,1)}, u32[]{:S(2)}) copy-start(bf16[1,512,1024]{2,1,0:T(8,128)(2,1)} %down_ref.1) | copy-start | bytes 3145732

commit v4 on v3

--- a/solution.py
+++ b/solution.py
@@ -145,42 +145,37 @@
             out_ref[i, g * group * used : (g + 1) * group * used, :] = block
 
 
-def expert_kernel(
-    slots_ref, up_ref, down_ref, up_other_hbm, down_other_hbm,
-    out_ref, normed_ref, hidden_ref, sum_ref, up_other_ref, down_other_ref, sems,
-):
-    parts, slots, shard = slots_ref.shape
-    width, units = up_ref.shape[1:]
-    copies = []
-    for source, target in ((up_other_hbm, up_other_ref), (down_other_hbm, down_other_ref)):
-        rows = source.shape[1] // 4
-        for g in range(4):
-            at = (0, slice(g * rows, (g + 1) * rows))
-            copies.append(pltpu.make_async_copy(source.at[at], target.at[at], sems.at[len(copies)]))
-    for copy in copies:
-        copy.start()
+def norm_kernel(slots_ref, up_hbm, normed_ref, up_ref, sem):
+    copy = pltpu.make_async_copy(up_hbm, up_ref, sem)
+    copy.start()
+    parts, slots, _ = slots_ref.shape
     block = slots // 3
     for g in range(slots // block):
         at = slice(g * block, (g + 1) * block)
         normed_ref[at, :] = normed_blocks([slots_ref[i, at, :].astype(F32) for i in range(parts)])
+    copy.wait()
+
+
+def own_half_kernel(normed_ref, up_ref, down_ref, sum_ref, hidden_ref):
+    units, width = down_ref.shape[1:]
     wide = 256
-
-    def hide(ref):
-        for n in range(0, units, wide):
-            hidden_ref[:, n : n + wide] = jax.nn.relu(dot(normed_ref[...], ref[0, :, n : n + wide])).astype(BF16)
-
-    hide(up_ref)
-    for i in range(parts):
-        at = slice(i * shard, (i + 1) * shard)
+    for n in range(0, units, wide):
+        at = slice(n, n + wide)
+        hidden_ref[:, at] = jax.nn.relu(dot(normed_ref[...], up_ref[0, :, at])).astype(BF16)
+    for n in range(0, width, wide):
+        at = slice(n, n + wide)
         sum_ref[:, at] = dot(hidden_ref[...], down_ref[0, :, at])
-    for copy in copies[:4]:
-        copy.wait()
-    hide(up_other_ref)
-    for copy in copies[4:]:
-        copy.wait()
-    for i in range(parts):
-        at = slice(i * shard, (i + 1) * shard)
-        out_ref[i] = (sum_ref[:, at] + dot(hidden_ref[...], down_other_ref[0, :, at])).astype(BF16)
+
+
+def other_half_kernel(normed_ref, sum_ref, up_ref, down_ref, out_ref, hidden_ref):
+    units, width = down_ref.shape[1:]
+    wide = width // out_ref.shape[0]
+    for n in range(0, units, wide):
+        at = slice(n, n + wide)
+        hidden_ref[:, at] = jax.nn.relu(dot(normed_ref[...], up_ref[0, :, at])).astype(BF16)
+    for i in range(out_ref.shape[0]):
+        at = slice(i * wide, (i + 1) * wide)
+        out_ref[i] = (sum_ref[:, at] + dot(hidden_ref[...], down_ref[0, :, at])).astype(BF16)
 
 
 def sum_kernel(used, parts_ref, out_ref):
@@ -235,7 +230,6 @@
         gates.transpose(0, 2, 1),
         cost=(10**9, 10**7),
     )
-    gathered, up_other, down_other = lax.optimization_barrier((gathered, up_other, down_other))
     middle, packed = call(
         functools.partial(attend_kernel, prefix),
         (shape((total, shard), BF16), shape((experts * PAD, shard), BF16)),
@@ -250,24 +244,33 @@
     arrived = exchange(packed.reshape(experts, PAD, shard), "yz").reshape(experts * PAD, shard)
     (spread,) = call(functools.partial(spread_kernel, used), [shape((parts, slots, shard), BF16)], arrived)
     whole = exchange(spread, "x")
-    (share,) = call(
-        expert_kernel,
-        [shape((parts, slots, shard), BF16)],
+    normed, up_own = call(
+        norm_kernel,
+        [shape((slots, width), BF16), shape(w_up.shape, BF16)],
         whole,
         w_up,
+        cost=(10**9, 10**7),
+        in_hbm=(1,),
+        scratch=[pltpu.SemaphoreType.DMA],
+    )
+    (half,) = call(
+        own_half_kernel,
+        [shape((slots, width), F32)],
+        normed,
+        up_own,
         w_down,
+        cost=(10**11, 10**7),
+        scratch=[pltpu.VMEM((slots, hidden), BF16)],
+    )
+    (share,) = call(
+        other_half_kernel,
+        [shape((parts, slots, shard), BF16)],
+        normed,
+        half,
         up_other,
         down_other,
-        cost=(8 * slots * width * hidden, 6 * 10**6),
-        in_hbm=(3, 4),
-        scratch=[
-            pltpu.VMEM((slots, width), BF16),
-            pltpu.VMEM((slots, hidden), BF16),
-            pltpu.VMEM((slots, width), F32),
-            pltpu.VMEM(w_up.shape, BF16),
-            pltpu.VMEM(w_down.shape, BF16),
-            pltpu.SemaphoreType.DMA((8,)),
-        ],
+        cost=(4 * slots * width * hidden, 6 * 10**6),
+        scratch=[pltpu.VMEM((slots, hidden), BF16)],
     )
     pieces = exchange(share, "x")
     (summed,) = call(functools.partial(sum_kernel, used), [shape((experts * PAD, shard), BF16)], pieces)

time: 89.7 us -> 86.8 us (0.968)
  blocking collectives: 67.2 us -> 54.4 us
  waiting for transfers between devices: 5.04 us -> 10.6 us
  starting transfers between devices: 8.61 us -> 12.1 us
    all_to_all x4 -> x3, blocking collectives: 67.2 us -> 54.4 us  [exchange(): lax.all_to_all(values, axis, split_axis=0, concat_axis=0, tiled=True, axi...]
    all_to_all x1 -> x2, waiting for transfers between devices: 5.03 us -> 10.6 us  [exchange(): lax.all_to_all(values, axis, split_axis=0, concat_axis=0, tiled=True, axi...]
    all_to_all x1 -> x2, starting transfers between devices: 4.29 us -> 7.79 us  [exchange(): lax.all_to_all(values, axis, split_axis=0, concat_axis=0, tiled=True, axi...]
    pallas_call x7 -> x9, Pallas kernels: 7.39 us -> 8.13 us  [call(): pl.pallas_call(kernel, out_shape=outs, in_specs=[pl.BlockSpec(memory_spac...]
  transfers between devices with their start and end apart: 3 -> 4, of which waited for: 1 -> 2; matrix products, arithmetic and copies ran while one was open for 0% -> 0% of each run, Pallas kernels for 2% -> 4%
where the time goes in v4:
time: 86.8 us; the launch traced here: 86.3 us
  blocking collectives  54.4 us (63%)
  starting transfers between devices  12.1 us (14%)
  waiting for transfers between devices  10.6 us (12%)
  Pallas kernels  8.13 us (9%)
  local copies, waits for them, and re-layouts  0.98 us (1%)
    all_to_all x3, blocking collectives, exchange(): lax.all_to_all(values, axis, split_axis=0, concat_axis=0, tiled=True, axi...  54.4 us
    all_to_all x2, waiting for transfers between devices, exchange(): lax.all_to_all(values, axis, split_axis=0, concat_axis=0, tiled=True, axi...  10.6 us
    pallas_call x9, Pallas kernels, call(): pl.pallas_call(kernel, out_shape=outs, in_specs=[pl.BlockSpec(memory_spac...  8.13 us
    all_to_all x2, starting transfers between devices, exchange(): lax.all_to_all(values, axis, split_axis=0, concat_axis=0, tiled=True, axi...  7.79 us
    ppermute x1, starting transfers between devices, shards(): down_other = lax.ppermute(w_down, 'core', swap)  2.41 us
    ppermute x1, starting transfers between devices, shards(): up_other = lax.ppermute(w_up, 'core', swap)  1.92 us
  transfers between devices with their start and end apart: 4, of which 2 were waited for; matrix products, arithmetic and copies ran while one was open for 0% of the time, Pallas kernels for 4%

profile of v4, /device:TPU:8, one launch (start us, length us, event | category | flops | bytes accessed | tf_op | source)
XLA Modules:
  0.0 86.3 jit_solution(16539854926682949585)
XLA Ops:
  0.0 0.0 copy-start.2
  0.0 0.7 copy-done.2
  0.7 0.6 shard_map.82
  1.4 4.3 %all-to-all-start = ((bf16[4,48,256]{2,1,0:T(8,128)(2,1)}), bf16[4,48,256]{2,1,0:T(8,128)(2,1)S(1)}, u32[]{:S(2)}, u32[]{:S(2)}) async-start(bf16[4,48,256]{2,1,0:T(8,128)(2,1)} %shard_map.82), calls=%async_computation | async-start | bytes 196608 | tf_op jit(solution)/shard_map/all_to_all | solution.py:211
  5.7 0.0 copy-done.5
  5.7 0.0 copy-done.6
  5.7 0.0 copy-done.7
  5.7 0.0 copy-start
  5.7 0.0 copy-start.1
  5.7 0.0 copy-start.3
  5.7 0.7 shard_map.83
  6.5 5.0 %all-to-all-done.gathered_ref = bf16[4,48,256]{2,1,0:T(8,128)(2,1)S(1)} async-done(((bf16[4,48,256]{2,1,0:T(8,128)(2,1)}), bf16[4,48,256]{2,1,0:T(8,128)(2,1)S(1)}, u32[]{:S(2)}, u32[]{:S(2)}) %all-to-all-start) | async-done | bytes 98336 | tf_op jit(solution)/shard_map/all_to_all | solution.py:211
  11.5 0.0 copy-done
  11.5 0.0 copy-done.1
  11.5 0.0 copy-done.3
  11.5 1.2 %shard_map.84 = (bf16[48,256]{1,0:T(8,128)(2,1)S(1)}, bf16[512,256]{1,0:T(8,128)(2,1)S(1)}) custom-call(bf16[4,48,256]{2,1,0:T(8,128)(2,1)S(1)} %all-to-all-done.gathered_ref, bf16[48,256]{1,0:T(8,128)(2,1)S(1)} %bitcast.15, bf16[3,1024,256]{2,1,0:T(8,128)(2,1)S(1)} %bitcast.9, bf16[16,2,64,256]{3,2,1,0:T(8,128)(2,1)S(1)} %copy-done.1, ...), custom_call_target="tpu_custom_call" | custom-call | flops 75497472 | bytes 3000000 | tf_op jit(solution)/shard_map/pallas_call | solution.py:35
  12.7 24.2 %all_to_all.25 = bf16[64,8,256]{2,1,0:T(8,128)(2,1)S(1)} all-to-all(bf16[64,8,256]{2,1,0:T(8,128)(2,1)S(1)} %bitcast.13), channel_id=1, replica_groups={{72,74,76,78,80,82,84,86,88,90,92,94,96,98,100,102,104,106,108,110,112,..., dimensions={0} | all-to-all | bytes 524288 | tf_op jit(solution)/shard_map/all_to_all | solution.py:211
  37.0 1.1 %shard_map.85 = bf16[4,384,256]{2,1,0:T(8,128)(2,1)} custom-call(bf16[512,256]{1,0:T(8,128)(2,1)S(1)} %bitcast.11), custom_call_target="tpu_custom_call" | custom-call | tf_op jit(solution)/shard_map/pallas_call | solution.py:35
  38.1 3.5 %all-to-all-start.2 = ((bf16[4,384,256]{2,1,0:T(8,128)(2,1)}), bf16[4,384,256]{2,1,0:T(8,128)(2,1)S(1)}, u32[]{:S(2)}, u32[]{:S(2)}) async-start(bf16[4,384,256]{2,1,0:T(8,128)(2,1)} %shard_map.85), calls=%async_computation.2 | async-start | bytes 1572864 | tf_op jit(solution)/shard_map/all_to_all | solution.py:211
  41.6 1.9 %collective-permute-start = (bf16[1,1024,512]{2,1,0:T(8,128)(2,1)}, bf16[1,1024,512]{2,1,0:T(8,128)(2,1)S(1)}, u32[]{:S(2)}, u32[]{:S(2)}) collective-permute-start(bf16[1,1024,512]{2,1,0:T(8,128)(2,1)} %up_hbm.1), channel_id=1, source_target_pairs={{0,1},{1,0},{2,3},{3,2},{4,5},{5,4},{6,7},{7,6},{8,9},{9,8},{10,11... | collective-permute-start | bytes 3145736 | tf_op jit(solution)/shard_map/ppermute | solution.py:218
  43.5 2.4 %collective-permute-start.1 = (bf16[1,512,1024]{2,1,0:T(8,128)(2,1)}, bf16[1,512,1024]{2,1,0:T(8,128)(2,1)S(1)}, u32[]{:S(2)}, u32[]{:S(2)}) collective-permute-start(bf16[1,512,1024]{2,1,0:T(8,128)(2,1)} %down_ref.1), channel_id=1, source_target_pairs={{0,1},{1,0},{2,3},{3,2},{4,5},{5,4},{6,7},{7,6},{8,9},{9,8},{10,11... | collective-permute-start | bytes 3145736 | tf_op jit(solution)/shard_map/ppermute | solution.py:219
  45.9 5.5 %all-to-all-done.2.slots_ref = bf16[4,384,256]{2,1,0:T(8,128)(2,1)S(1)} async-done(((bf16[4,384,256]{2,1,0:T(8,128)(2,1)}), bf16[4,384,256]{2,1,0:T(8,128)(2,1)S(1)}, u32[]{:S(2)}, u32[]{:S(2)}) %all-to-all-start.2) | async-done | bytes 786464 | tf_op jit(solution)/shard_map/all_to_all | solution.py:211
  51.4 1.3 %shard_map.86 = (bf16[384,1024]{1,0:T(8,128)(2,1)S(1)}, bf16[1,1024,512]{2,1,0:T(8,128)(2,1)S(1)}) custom-call(bf16[4,384,256]{2,1,0:T(8,128)(2,1)S(1)} %all-to-all-done.2.slots_ref, bf16[1,1024,512]{2,1,0:T(8,128)(2,1)} %up_hbm.1), custom_call_target="tpu_custom_call" | custom-call | flops 1000000000 | bytes 10000000 | tf_op jit(solution)/shard_map/pallas_call | solution.py:35
  52.8 0.2 copy-done.4
  53.0 1.0 %shard_map.87.sum_ref = f32[384,1024]{1,0:T(8,128)S(1)} custom-call(bf16[384,1024]{1,0:T(8,128)(2,1)S(1)} %get-tuple-element.17.normed_ref, bf16[1,1024,512]{2,1,0:T(8,128)(2,1)S(1)} %get-tuple-element.18.up_ref, bf16[1,512,1024]{2,1,0:T(8,128)(2,1)S(1)} %copy-done.4), custom_call_target="tpu_custom_call" | custom-call | flops 99999997952 | bytes 10000000 | tf_op jit(solution)/shard_map/pallas_call | solution.py:35
  54.0 0.0 collective-permute-done.up_ref
  54.0 0.0 collective-permute-done.1.down_ref
  54.0 1.0 %shard_map.88 = bf16[4,384,256]{2,1,0:T(8,128)(2,1)S(1)} custom-call(bf16[384,1024]{1,0:T(8,128)(2,1)S(1)} %get-tuple-element.17.normed_ref, f32[384,1024]{1,0:T(8,128)S(1)} %shard_map.87.sum_ref, bf16[1,1024,512]{2,1,0:T(8,128)(2,1)S(1)} %collective-permute-done.up_ref, bf16[1,512,1024]{2,1,0:T(8,128)(2,1)S(1)} %collective-permute-done.1.down_ref), custom_call_target="tpu_custom_call" | custom-call | flops 805306368 | bytes 6000000 | tf_op jit(solution)/shard_map/pallas_call | solution.py:35
  55.1 11.9 %all_to_all.26.parts_ref = bf16[4,384,256]{2,1,0:T(8,128)(2,1)S(1)} all-to-all(bf16[4,384,256]{2,1,0:T(8,128)(2,1)S(1)} %shard_map.88), channel_id=1, replica_groups=mesh['x'=4,'yz'=64,'core'=2] {'x'}, dimensions={0} | all-to-all | bytes 1572864 | tf_op jit(solution)/shard_map/all_to_all | solution.py:211
  67.0 0.3 shard_map.89
  67.2 18.3 %all_to_all.27 = bf16[64,8,256]{2,1,0:T(8,128)(2,1)S(1)} all-to-all(bf16[64,8,256]{2,1,0:T(8,128)(2,1)S(1)} %bitcast.12), channel_id=1, replica_groups={{72,74,76,78,80,82,84,86,88,90,92,94,96,98,100,102,104,106,108,110,112,..., dimensions={0} | all-to-all | bytes 524288 | tf_op jit(solution)/shard_map/all_to_all | solution.py:211
  85.5 0.8 shard_map.90
  (4 shorter events, 0.0 us)
Async XLA Ops:
  0.0 0.7 copy-start.2
  0.7 4.9 %copy-start.5 = (s32[3,16,2]{1,2,0:T(2,128)S(1)}, s32[3,16,2]{1,2,0:T(2,128)}, u32[]{:S(2)}) copy-start(s32[3,16,2]{1,2,0:T(2,128)} %param.14) | copy-start | bytes 1156
  0.7 4.9 %copy-start.6 = (f32[3,16,2]{1,2,0:T(2,128)S(1)}, f32[3,16,2]{1,2,0:T(2,128)}, u32[]{:S(2)}) copy-start(f32[3,16,2]{1,2,0:T(2,128)} %param.15) | copy-start | bytes 1156
  0.7 4.9 %copy-start.7 = (s32[3,16]{1,0:T(4,128)S(1)}, s32[3,16]{1,0:T(4,128)}, u32[]{:S(2)}) copy-start(s32[3,16]{1,0:T(4,128)} %parents_ref.1) | copy-start | bytes 580
  1.4 10.1 %all-to-all-start = ((bf16[4,48,256]{2,1,0:T(8,128)(2,1)}), bf16[4,48,256]{2,1,0:T(8,128)(2,1)S(1)}, u32[]{:S(2)}, u32[]{:S(2)}) async-start(bf16[4,48,256]{2,1,0:T(8,128)(2,1)} %shard_map.82), calls=%async_computation | async-start | bytes 196608 | tf_op jit(solution)/shard_map/all_to_all | solution.py:211
  5.7 5.8 %copy-start = (bf16[1024,3,256]{2,0,1:T(8,128)(2,1)S(1)}, bf16[1024,3,256]{2,0,1:T(8,128)(2,1)}, u32[]{:S(2)}) copy-start(bf16[1024,3,256]{2,0,1:T(8,128)(2,1)} %param.10) | copy-start | bytes 4718596
  5.7 5.8 %copy-start.1 = (bf16[16,2,64,256]{3,2,1,0:T(8,128)(2,1)S(1)}, bf16[16,2,64,256]{3,2,1,0:T(8,128)(2,1)}, u32[]{:S(2)}) copy-start(bf16[16,2,64,256]{3,2,1,0:T(8,128)(2,1)} %cache_ref.1) | copy-start | bytes 3145732
  5.7 5.8 %copy-start.3 = (bf16[3,16,256]{2,1,0:T(8,128)(2,1)S(1)}, bf16[3,16,256]{2,1,0:T(8,128)(2,1)}, u32[]{:S(2)}) copy-start(bf16[3,16,256]{2,1,0:T(8,128)(2,1)} %param.8) | copy-start | bytes 73732
  38.1 13.4 %all-to-all-start.2 = ((bf16[4,384,256]{2,1,0:T(8,128)(2,1)}), bf16[4,384,256]{2,1,0:T(8,128)(2,1)S(1)}, u32[]{:S(2)}, u32[]{:S(2)}) async-start(bf16[4,384,256]{2,1,0:T(8,128)(2,1)} %shard_map.85), calls=%async_computation.2 | async-start | bytes 1572864 | tf_op jit(solution)/shard_map/all_to_all | solution.py:211
  41.6 12.4 %collective-permute-start = (bf16[1,1024,512]{2,1,0:T(8,128)(2,1)}, bf16[1,1024,512]{2,1,0:T(8,128)(2,1)S(1)}, u32[]{:S(2)}, u32[]{:S(2)}) collective-permute-start(bf16[1,1024,512]{2,1,0:T(8,128)(2,1)} %up_hbm.1), channel_id=1, source_target_pairs={{0,1},{1,0},{2,3},{3,2},{4,5},{5,4},{6,7},{7,6},{8,9},{9,8},{10,11... | collective-permute-start | bytes 3145736 | tf_op jit(solution)/shard_map/ppermute | solution.py:218
  43.5 10.5 %collective-permute-start.1 = (bf16[1,512,1024]{2,1,0:T(8,128)(2,1)}, bf16[1,512,1024]{2,1,0:T(8,128)(2,1)S(1)}, u32[]{:S(2)}, u32[]{:S(2)}) collective-permute-start(bf16[1,512,1024]{2,1,0:T(8,128)(2,1)} %down_ref.1), channel_id=1, source_target_pairs={{0,1},{1,0},{2,3},{3,2},{4,5},{5,4},{6,7},{7,6},{8,9},{9,8},{10,11... | collective-permute-start | bytes 3145736 | tf_op jit(solution)/shard_map/ppermute | solution.py:219
  51.4 1.5 %copy-start.4 = (bf16[1,512,1024]{2,1,0:T(8,128)(2,1)S(1)}, bf16[1,512,1024]{2,1,0:T(8,128)(2,1)}, u32[]{:S(2)}) copy-start(bf16[1,512,1024]{2,1,0:T(8,128)(2,1)} %down_ref.1) | copy-start | bytes 3145732

commit v5 on v4

--- a/solution.py
+++ b/solution.py
@@ -41,6 +41,10 @@
         compiler_params=pltpu.CompilerParams(vmem_limit_bytes=limit * 1024 * 1024),
         cost_estimate=pl.CostEstimate(flops=flops, bytes_accessed=nbytes, transcendentals=0),
     )(*args)
+
+
+def place_of(device, parts):
+    return (device + parts // 2) % parts
 
 
 def copies_kernel(token_ref, out_ref):
@@ -119,7 +123,7 @@
     parts = gathered_ref.shape[0]
     total, shard = token_ref.shape
     rows = cache_ref.shape[0]
-    normed = normed_blocks([gathered_ref[i].astype(F32) for i in range(parts)])
+    normed = normed_blocks([gathered_ref[place_of(i, parts)].astype(F32) for i in range(parts)])
     query, key, value = (dot(normed, w_ref[j]).astype(BF16) for j in range(3))
     bias_old = bias_ref[:, : rows * prefix]
     bias_new = bias_ref[:, rows * prefix : rows * prefix + total]
@@ -152,7 +156,7 @@
     block = slots // 3
     for g in range(slots // block):
         at = slice(g * block, (g + 1) * block)
-        normed_ref[at, :] = normed_blocks([slots_ref[i, at, :].astype(F32) for i in range(parts)])
+        normed_ref[at, :] = normed_blocks([slots_ref[place_of(i, parts), at, :].astype(F32) for i in range(parts)])
     copy.wait()
 
 
@@ -175,7 +179,7 @@
         hidden_ref[:, at] = jax.nn.relu(dot(normed_ref[...], up_ref[0, :, at])).astype(BF16)
     for i in range(out_ref.shape[0]):
         at = slice(i * wide, (i + 1) * wide)
-        out_ref[i] = (sum_ref[:, at] + dot(hidden_ref[...], down_ref[0, :, at])).astype(BF16)
+        out_ref[place_of(i, out_ref.shape[0])] = (sum_ref[:, at] + dot(hidden_ref[...], down_ref[0, :, at])).astype(BF16)
 
 
 def sum_kernel(used, parts_ref, out_ref):
@@ -189,8 +193,9 @@
 
 
 def combine_kernel(middle_ref, returned_ref, high_ref, low_ref, out_ref):
-    returned = returned_ref[...]
-    added = dot(high_ref[...], returned) + dot(low_ref[...], returned)
+    total = middle_ref.shape[0]
+    both = dot(jnp.concatenate([high_ref[...], low_ref[...]], axis=0), returned_ref[...])
+    added = both[:total] + both[total:]
     out_ref[...] = (middle_ref[...].astype(F32) + added).astype(BF16)
 
 
@@ -207,7 +212,7 @@
     order = [[(p + first_expert) % experts for p in range(experts)]]
 
     def exchange(values, axis):
-        groups = order if axis == "yz" else None
+        groups = order if axis == "yz" else [[place_of(p, parts) for p in range(parts)]]
         return lax.all_to_all(values, axis, split_axis=0, concat_axis=0, tiled=True, axis_index_groups=groups)
 
     tokens = embeds.reshape(total, shard)

time: 86.8 us -> 86.4 us (level)
  waiting for transfers between devices: 10.6 us -> 4.58 us
  starting transfers between devices: 12.1 us -> 17 us
    all_to_all x2, waiting for transfers between devices: 10.6 us -> 4.58 us  [exchange(): lax.all_to_all(values, axis, split_axis=0, concat_axis=0, tiled=True, axi...]
    all_to_all x2, starting transfers between devices: 7.79 us -> 12.7 us  [exchange(): lax.all_to_all(values, axis, split_axis=0, concat_axis=0, tiled=True, axi...]
where the time goes in v5:
time: 86.4 us; the launch traced here: 85.7 us
  blocking collectives  54.8 us (63%)
  starting transfers between devices  17 us (20%)
  Pallas kernels  8.11 us (9%)
  waiting for transfers between devices  4.58 us (5%)
  local copies, waits for them, and re-layouts  0.98 us (1%)
    all_to_all x3, blocking collectives, exchange(): lax.all_to_all(values, axis, split_axis=0, concat_axis=0, tiled=True, axi...  54.8 us
    all_to_all x2, starting transfers between devices, exchange(): lax.all_to_all(values, axis, split_axis=0, concat_axis=0, tiled=True, axi...  12.7 us
    pallas_call x9, Pallas kernels, call(): pl.pallas_call(kernel, out_shape=outs, in_specs=[pl.BlockSpec(memory_spac...  8.11 us
    all_to_all x2, waiting for transfers between devices, exchange(): lax.all_to_all(values, axis, split_axis=0, concat_axis=0, tiled=True, axi...  4.58 us
    ppermute x1, starting transfers between devices, shards(): down_other = lax.ppermute(w_down, 'core', swap)  2.41 us
    ppermute x1, starting transfers between devices, shards(): up_other = lax.ppermute(w_up, 'core', swap)  1.91 us
  transfers between devices with their start and end apart: 4, of which 2 were waited for; matrix products, arithmetic and copies ran while one was open for 0% of the time, Pallas kernels for 4%

profile of v5, /device:TPU:8, one launch (start us, length us, event | category | flops | bytes accessed | tf_op | source)
XLA Modules:
  0.0 85.7 jit_solution(3250620706325365212)
XLA Ops:
  0.0 0.0 copy-start.2
  0.0 0.7 copy-done.2
  0.7 0.6 shard_map.82
  1.4 6.3 %all-to-all-start = ((bf16[4,48,256]{2,1,0:T(8,128)(2,1)}), bf16[4,48,256]{2,1,0:T(8,128)(2,1)S(1)}, u32[]{:S(2)}, u32[]{:S(2)}) async-start(bf16[4,48,256]{2,1,0:T(8,128)(2,1)} %shard_map.82), calls=%async_computation | async-start | bytes 196608 | tf_op jit(solution)/shard_map/all_to_all | solution.py:216
  7.7 0.0 copy-done.5
  7.7 0.0 copy-done.6
  7.7 0.0 copy-done.7
  7.7 0.0 copy-start
  7.7 0.0 copy-start.1
  7.7 0.0 copy-start.3
  7.7 0.7 shard_map.83
  8.5 1.8 %all-to-all-done.gathered_ref = bf16[4,48,256]{2,1,0:T(8,128)(2,1)S(1)} async-done(((bf16[4,48,256]{2,1,0:T(8,128)(2,1)}), bf16[4,48,256]{2,1,0:T(8,128)(2,1)S(1)}, u32[]{:S(2)}, u32[]{:S(2)}) %all-to-all-start) | async-done | bytes 98336 | tf_op jit(solution)/shard_map/all_to_all | solution.py:216
  10.3 0.0 copy-done
  10.3 0.0 copy-done.1
  10.3 0.0 copy-done.3
  10.3 1.2 %shard_map.84 = (bf16[48,256]{1,0:T(8,128)(2,1)S(1)}, bf16[512,256]{1,0:T(8,128)(2,1)S(1)}) custom-call(bf16[4,48,256]{2,1,0:T(8,128)(2,1)S(1)} %all-to-all-done.gathered_ref, bf16[48,256]{1,0:T(8,128)(2,1)S(1)} %bitcast.15, bf16[3,1024,256]{2,1,0:T(8,128)(2,1)S(1)} %bitcast.9, bf16[16,2,64,256]{3,2,1,0:T(8,128)(2,1)S(1)} %copy-done.1, ...), custom_call_target="tpu_custom_call" | custom-call | flops 75497472 | bytes 3000000 | tf_op jit(solution)/shard_map/pallas_call | solution.py:35
  11.5 24.7 %all_to_all.25 = bf16[64,8,256]{2,1,0:T(8,128)(2,1)S(1)} all-to-all(bf16[64,8,256]{2,1,0:T(8,128)(2,1)S(1)} %bitcast.13), channel_id=1, replica_groups={{72,74,76,78,80,82,84,86,88,90,92,94,96,98,100,102,104,106,108,110,112,..., dimensions={0} | all-to-all | bytes 524288 | tf_op jit(solution)/shard_map/all_to_all | solution.py:216
  36.3 1.1 %shard_map.85 = bf16[4,384,256]{2,1,0:T(8,128)(2,1)} custom-call(bf16[512,256]{1,0:T(8,128)(2,1)S(1)} %bitcast.11), custom_call_target="tpu_custom_call" | custom-call | tf_op jit(solution)/shard_map/pallas_call | solution.py:35
  37.4 6.4 %all-to-all-start.2 = ((bf16[4,384,256]{2,1,0:T(8,128)(2,1)}), bf16[4,384,256]{2,1,0:T(8,128)(2,1)S(1)}, u32[]{:S(2)}, u32[]{:S(2)}) async-start(bf16[4,384,256]{2,1,0:T(8,128)(2,1)} %shard_map.85), calls=%async_computation.2 | async-start | bytes 1572864 | tf_op jit(solution)/shard_map/all_to_all | solution.py:216
  43.8 1.9 %collective-permute-start = (bf16[1,1024,512]{2,1,0:T(8,128)(2,1)}, bf16[1,1024,512]{2,1,0:T(8,128)(2,1)S(1)}, u32[]{:S(2)}, u32[]{:S(2)}) collective-permute-start(bf16[1,1024,512]{2,1,0:T(8,128)(2,1)} %up_hbm.1), channel_id=1, source_target_pairs={{0,1},{1,0},{2,3},{3,2},{4,5},{5,4},{6,7},{7,6},{8,9},{9,8},{10,11... | collective-permute-start | bytes 3145736 | tf_op jit(solution)/shard_map/ppermute | solution.py:223
  45.7 2.4 %collective-permute-start.1 = (bf16[1,512,1024]{2,1,0:T(8,128)(2,1)}, bf16[1,512,1024]{2,1,0:T(8,128)(2,1)S(1)}, u32[]{:S(2)}, u32[]{:S(2)}) collective-permute-start(bf16[1,512,1024]{2,1,0:T(8,128)(2,1)} %down_ref.1), channel_id=1, source_target_pairs={{0,1},{1,0},{2,3},{3,2},{4,5},{5,4},{6,7},{7,6},{8,9},{9,8},{10,11... | collective-permute-start | bytes 3145736 | tf_op jit(solution)/shard_map/ppermute | solution.py:224
  48.1 2.8 %all-to-all-done.2.slots_ref = bf16[4,384,256]{2,1,0:T(8,128)(2,1)S(1)} async-done(((bf16[4,384,256]{2,1,0:T(8,128)(2,1)}), bf16[4,384,256]{2,1,0:T(8,128)(2,1)S(1)}, u32[]{:S(2)}, u32[]{:S(2)}) %all-to-all-start.2) | async-done | bytes 786464 | tf_op jit(solution)/shard_map/all_to_all | solution.py:216
  50.9 1.3 %shard_map.86 = (bf16[384,1024]{1,0:T(8,128)(2,1)S(1)}, bf16[1,1024,512]{2,1,0:T(8,128)(2,1)S(1)}) custom-call(bf16[4,384,256]{2,1,0:T(8,128)(2,1)S(1)} %all-to-all-done.2.slots_ref, bf16[1,1024,512]{2,1,0:T(8,128)(2,1)} %up_hbm.1), custom_call_target="tpu_custom_call" | custom-call | flops 1000000000 | bytes 10000000 | tf_op jit(solution)/shard_map/pallas_call | solution.py:35
  52.2 0.2 copy-done.4
  52.4 1.0 %shard_map.87.sum_ref = f32[384,1024]{1,0:T(8,128)S(1)} custom-call(bf16[384,1024]{1,0:T(8,128)(2,1)S(1)} %get-tuple-element.17.normed_ref, bf16[1,1024,512]{2,1,0:T(8,128)(2,1)S(1)} %get-tuple-element.18.up_ref, bf16[1,512,1024]{2,1,0:T(8,128)(2,1)S(1)} %copy-done.4), custom_call_target="tpu_custom_call" | custom-call | flops 99999997952 | bytes 10000000 | tf_op jit(solution)/shard_map/pallas_call | solution.py:35
  53.5 0.0 collective-permute-done.up_ref
  53.5 0.0 collective-permute-done.1.down_ref
  53.5 1.0 %shard_map.88 = bf16[4,384,256]{2,1,0:T(8,128)(2,1)S(1)} custom-call(bf16[384,1024]{1,0:T(8,128)(2,1)S(1)} %get-tuple-element.17.normed_ref, f32[384,1024]{1,0:T(8,128)S(1)} %shard_map.87.sum_ref, bf16[1,1024,512]{2,1,0:T(8,128)(2,1)S(1)} %collective-permute-done.up_ref, bf16[1,512,1024]{2,1,0:T(8,128)(2,1)S(1)} %collective-permute-done.1.down_ref), custom_call_target="tpu_custom_call" | custom-call | flops 805306368 | bytes 6000000 | tf_op jit(solution)/shard_map/pallas_call | solution.py:35
  54.5 11.7 %all_to_all.26.parts_ref = bf16[4,384,256]{2,1,0:T(8,128)(2,1)S(1)} all-to-all(bf16[4,384,256]{2,1,0:T(8,128)(2,1)S(1)} %shard_map.88), channel_id=1, replica_groups={{256,384,0,128},{257,385,1,129},{258,386,2,130},{259,387,3,131},{260,38..., dimensions={0} | all-to-all | bytes 1572864 | tf_op jit(solution)/shard_map/all_to_all | solution.py:216
  66.2 0.3 shard_map.89
  66.5 18.4 %all_to_all.27 = bf16[64,8,256]{2,1,0:T(8,128)(2,1)S(1)} all-to-all(bf16[64,8,256]{2,1,0:T(8,128)(2,1)S(1)} %bitcast.12), channel_id=1, replica_groups={{72,74,76,78,80,82,84,86,88,90,92,94,96,98,100,102,104,106,108,110,112,..., dimensions={0} | all-to-all | bytes 524288 | tf_op jit(solution)/shard_map/all_to_all | solution.py:216
  84.9 0.8 shard_map.90
  (4 shorter events, 0.0 us)
Async XLA Ops:
  0.0 0.7 copy-start.2
  0.7 7.0 %copy-start.5 = (s32[3,16,2]{1,2,0:T(2,128)S(1)}, s32[3,16,2]{1,2,0:T(2,128)}, u32[]{:S(2)}) copy-start(s32[3,16,2]{1,2,0:T(2,128)} %param.14) | copy-start | bytes 1156
  0.7 7.0 %copy-start.6 = (f32[3,16,2]{1,2,0:T(2,128)S(1)}, f32[3,16,2]{1,2,0:T(2,128)}, u32[]{:S(2)}) copy-start(f32[3,16,2]{1,2,0:T(2,128)} %param.15) | copy-start | bytes 1156
  0.7 7.0 %copy-start.7 = (s32[3,16]{1,0:T(4,128)S(1)}, s32[3,16]{1,0:T(4,128)}, u32[]{:S(2)}) copy-start(s32[3,16]{1,0:T(4,128)} %parents_ref.1) | copy-start | bytes 580
  1.4 8.9 %all-to-all-start = ((bf16[4,48,256]{2,1,0:T(8,128)(2,1)}), bf16[4,48,256]{2,1,0:T(8,128)(2,1)S(1)}, u32[]{:S(2)}, u32[]{:S(2)}) async-start(bf16[4,48,256]{2,1,0:T(8,128)(2,1)} %shard_map.82), calls=%async_computation | async-start | bytes 196608 | tf_op jit(solution)/shard_map/all_to_all | solution.py:216
  7.7 2.6 %copy-start = (bf16[1024,3,256]{2,0,1:T(8,128)(2,1)S(1)}, bf16[1024,3,256]{2,0,1:T(8,128)(2,1)}, u32[]{:S(2)}) copy-start(bf16[1024,3,256]{2,0,1:T(8,128)(2,1)} %param.10) | copy-start | bytes 4718596
  7.7 2.6 %copy-start.1 = (bf16[16,2,64,256]{3,2,1,0:T(8,128)(2,1)S(1)}, bf16[16,2,64,256]{3,2,1,0:T(8,128)(2,1)}, u32[]{:S(2)}) copy-start(bf16[16,2,64,256]{3,2,1,0:T(8,128)(2,1)} %cache_ref.1) | copy-start | bytes 3145732
  7.7 2.5 %copy-start.3 = (bf16[3,16,256]{2,1,0:T(8,128)(2,1)S(1)}, bf16[3,16,256]{2,1,0:T(8,128)(2,1)}, u32[]{:S(2)}) copy-start(bf16[3,16,256]{2,1,0:T(8,128)(2,1)} %param.8) | copy-start | bytes 73732
  37.4 13.5 %all-to-all-start.2 = ((bf16[4,384,256]{2,1,0:T(8,128)(2,1)}), bf16[4,384,256]{2,1,0:T(8,128)(2,1)S(1)}, u32[]{:S(2)}, u32[]{:S(2)}) async-start(bf16[4,384,256]{2,1,0:T(8,128)(2,1)} %shard_map.85), calls=%async_computation.2 | async-start | bytes 1572864 | tf_op jit(solution)/shard_map/all_to_all | solution.py:216
  43.8 9.7 %collective-permute-start = (bf16[1,1024,512]{2,1,0:T(8,128)(2,1)}, bf16[1,1024,512]{2,1,0:T(8,128)(2,1)S(1)}, u32[]{:S(2)}, u32[]{:S(2)}) collective-permute-start(bf16[1,1024,512]{2,1,0:T(8,128)(2,1)} %up_hbm.1), channel_id=1, source_target_pairs={{0,1},{1,0},{2,3},{3,2},{4,5},{5,4},{6,7},{7,6},{8,9},{9,8},{10,11... | collective-permute-start | bytes 3145736 | tf_op jit(solution)/shard_map/ppermute | solution.py:223
  45.7 7.8 %collective-permute-start.1 = (bf16[1,512,1024]{2,1,0:T(8,128)(2,1)}, bf16[1,512,1024]{2,1,0:T(8,128)(2,1)S(1)}, u32[]{:S(2)}, u32[]{:S(2)}) collective-permute-start(bf16[1,512,1024]{2,1,0:T(8,128)(2,1)} %down_ref.1), channel_id=1, source_target_pairs={{0,1},{1,0},{2,3},{3,2},{4,5},{5,4},{6,7},{7,6},{8,9},{9,8},{10,11... | collective-permute-start | bytes 3145736 | tf_op jit(solution)/shard_map/ppermute | solution.py:224
  50.9 1.5 %copy-start.4 = (bf16[1,512,1024]{2,1,0:T(8,128)(2,1)S(1)}, bf16[1,512,1024]{2,1,0:T(8,128)(2,1)}, u32[]{:S(2)}) copy-start(bf16[1,512,1024]{2,1,0:T(8,128)(2,1)} %down_ref.1) | copy-start | bytes 3145732

commit v6 on v5

--- a/solution.py
+++ b/solution.py
@@ -208,7 +208,7 @@
     slots = experts * used
     shape = jax.ShapeDtypeStruct
 
-    first_expert = experts // 2 + 4
+    first_expert = experts // 2 + 6
     order = [[(p + first_expert) % experts for p in range(experts)]]
 
     def exchange(values, axis):

time: 86.4 us -> 86.6 us (level)
  no operation moved by 1% of the time
where the time goes in v6:
time: 86.6 us; the launch traced here: 86 us
  blocking collectives  55 us (64%)
  starting transfers between devices  17 us (20%)
  Pallas kernels  8.11 us (9%)
  waiting for transfers between devices  4.76 us (5%)
  local copies, waits for them, and re-layouts  0.98 us (1%)
    all_to_all x3, blocking collectives, exchange(): lax.all_to_all(values, axis, split_axis=0, concat_axis=0, tiled=True, axi...  55 us
    all_to_all x2, starting transfers between devices, exchange(): lax.all_to_all(values, axis, split_axis=0, concat_axis=0, tiled=True, axi...  12.7 us
    pallas_call x9, Pallas kernels, call(): pl.pallas_call(kernel, out_shape=outs, in_specs=[pl.BlockSpec(memory_spac...  8.11 us
    all_to_all x2, waiting for transfers between devices, exchange(): lax.all_to_all(values, axis, split_axis=0, concat_axis=0, tiled=True, axi...  4.76 us
    ppermute x1, starting transfers between devices, shards(): down_other = lax.ppermute(w_down, 'core', swap)  2.41 us
    ppermute x1, starting transfers between devices, shards(): up_other = lax.ppermute(w_up, 'core', swap)  1.91 us
  transfers between devices with their start and end apart: 4, of which 2 were waited for; matrix products, arithmetic and copies ran while one was open for 0% of the time, Pallas kernels for 4%

profile of v6, /device:TPU:8, one launch (start us, length us, event | category | flops | bytes accessed | tf_op | source)
XLA Modules:
  0.0 86.0 jit_solution(5409349529528485437)
XLA Ops:
  0.0 0.0 copy-start.2
  0.0 0.7 copy-done.2
  0.7 0.6 shard_map.82
  1.4 6.3 %all-to-all-start = ((bf16[4,48,256]{2,1,0:T(8,128)(2,1)}), bf16[4,48,256]{2,1,0:T(8,128)(2,1)S(1)}, u32[]{:S(2)}, u32[]{:S(2)}) async-start(bf16[4,48,256]{2,1,0:T(8,128)(2,1)} %shard_map.82), calls=%async_computation | async-start | bytes 196608 | tf_op jit(solution)/shard_map/all_to_all | solution.py:216
  7.7 0.0 copy-done.5
  7.7 0.0 copy-done.6
  7.7 0.0 copy-done.7
  7.7 0.0 copy-start
  7.7 0.0 copy-start.1
  7.7 0.0 copy-start.3
  7.7 0.7 shard_map.83
  8.5 1.8 %all-to-all-done.gathered_ref = bf16[4,48,256]{2,1,0:T(8,128)(2,1)S(1)} async-done(((bf16[4,48,256]{2,1,0:T(8,128)(2,1)}), bf16[4,48,256]{2,1,0:T(8,128)(2,1)S(1)}, u32[]{:S(2)}, u32[]{:S(2)}) %all-to-all-start) | async-done | bytes 98336 | tf_op jit(solution)/shard_map/all_to_all | solution.py:216
  10.3 0.0 copy-done
  10.3 0.0 copy-done.1
  10.3 0.0 copy-done.3
  10.3 1.2 %shard_map.84 = (bf16[48,256]{1,0:T(8,128)(2,1)S(1)}, bf16[512,256]{1,0:T(8,128)(2,1)S(1)}) custom-call(bf16[4,48,256]{2,1,0:T(8,128)(2,1)S(1)} %all-to-all-done.gathered_ref, bf16[48,256]{1,0:T(8,128)(2,1)S(1)} %bitcast.15, bf16[3,1024,256]{2,1,0:T(8,128)(2,1)S(1)} %bitcast.9, bf16[16,2,64,256]{3,2,1,0:T(8,128)(2,1)S(1)} %copy-done.1, ...), custom_call_target="tpu_custom_call" | custom-call | flops 75497472 | bytes 3000000 | tf_op jit(solution)/shard_map/pallas_call | solution.py:35
  11.5 24.8 %all_to_all.25 = bf16[64,8,256]{2,1,0:T(8,128)(2,1)S(1)} all-to-all(bf16[64,8,256]{2,1,0:T(8,128)(2,1)S(1)} %bitcast.13), channel_id=1, replica_groups={{76,78,80,82,84,86,88,90,92,94,96,98,100,102,104,106,108,110,112,114,11..., dimensions={0} | all-to-all | bytes 524288 | tf_op jit(solution)/shard_map/all_to_all | solution.py:216
  36.3 1.1 %shard_map.85 = bf16[4,384,256]{2,1,0:T(8,128)(2,1)} custom-call(bf16[512,256]{1,0:T(8,128)(2,1)S(1)} %bitcast.11), custom_call_target="tpu_custom_call" | custom-call | tf_op jit(solution)/shard_map/pallas_call | solution.py:35
  37.4 6.4 %all-to-all-start.2 = ((bf16[4,384,256]{2,1,0:T(8,128)(2,1)}), bf16[4,384,256]{2,1,0:T(8,128)(2,1)S(1)}, u32[]{:S(2)}, u32[]{:S(2)}) async-start(bf16[4,384,256]{2,1,0:T(8,128)(2,1)} %shard_map.85), calls=%async_computation.2 | async-start | bytes 1572864 | tf_op jit(solution)/shard_map/all_to_all | solution.py:216
  43.8 1.9 %collective-permute-start = (bf16[1,1024,512]{2,1,0:T(8,128)(2,1)}, bf16[1,1024,512]{2,1,0:T(8,128)(2,1)S(1)}, u32[]{:S(2)}, u32[]{:S(2)}) collective-permute-start(bf16[1,1024,512]{2,1,0:T(8,128)(2,1)} %up_hbm.1), channel_id=1, source_target_pairs={{0,1},{1,0},{2,3},{3,2},{4,5},{5,4},{6,7},{7,6},{8,9},{9,8},{10,11... | collective-permute-start | bytes 3145736 | tf_op jit(solution)/shard_map/ppermute | solution.py:223
  45.7 2.4 %collective-permute-start.1 = (bf16[1,512,1024]{2,1,0:T(8,128)(2,1)}, bf16[1,512,1024]{2,1,0:T(8,128)(2,1)S(1)}, u32[]{:S(2)}, u32[]{:S(2)}) collective-permute-start(bf16[1,512,1024]{2,1,0:T(8,128)(2,1)} %down_ref.1), channel_id=1, source_target_pairs={{0,1},{1,0},{2,3},{3,2},{4,5},{5,4},{6,7},{7,6},{8,9},{9,8},{10,11... | collective-permute-start | bytes 3145736 | tf_op jit(solution)/shard_map/ppermute | solution.py:224
  48.2 3.0 %all-to-all-done.2.slots_ref = bf16[4,384,256]{2,1,0:T(8,128)(2,1)S(1)} async-done(((bf16[4,384,256]{2,1,0:T(8,128)(2,1)}), bf16[4,384,256]{2,1,0:T(8,128)(2,1)S(1)}, u32[]{:S(2)}, u32[]{:S(2)}) %all-to-all-start.2) | async-done | bytes 786464 | tf_op jit(solution)/shard_map/all_to_all | solution.py:216
  51.1 1.3 %shard_map.86 = (bf16[384,1024]{1,0:T(8,128)(2,1)S(1)}, bf16[1,1024,512]{2,1,0:T(8,128)(2,1)S(1)}) custom-call(bf16[4,384,256]{2,1,0:T(8,128)(2,1)S(1)} %all-to-all-done.2.slots_ref, bf16[1,1024,512]{2,1,0:T(8,128)(2,1)} %up_hbm.1), custom_call_target="tpu_custom_call" | custom-call | flops 1000000000 | bytes 10000000 | tf_op jit(solution)/shard_map/pallas_call | solution.py:35
  52.4 0.2 copy-done.4
  52.6 1.0 %shard_map.87.sum_ref = f32[384,1024]{1,0:T(8,128)S(1)} custom-call(bf16[384,1024]{1,0:T(8,128)(2,1)S(1)} %get-tuple-element.17.normed_ref, bf16[1,1024,512]{2,1,0:T(8,128)(2,1)S(1)} %get-tuple-element.18.up_ref, bf16[1,512,1024]{2,1,0:T(8,128)(2,1)S(1)} %copy-done.4), custom_call_target="tpu_custom_call" | custom-call | flops 99999997952 | bytes 10000000 | tf_op jit(solution)/shard_map/pallas_call | solution.py:35
  53.7 0.0 collective-permute-done.up_ref
  53.7 0.0 collective-permute-done.1.down_ref
  53.7 1.0 %shard_map.88 = bf16[4,384,256]{2,1,0:T(8,128)(2,1)S(1)} custom-call(bf16[384,1024]{1,0:T(8,128)(2,1)S(1)} %get-tuple-element.17.normed_ref, f32[384,1024]{1,0:T(8,128)S(1)} %shard_map.87.sum_ref, bf16[1,1024,512]{2,1,0:T(8,128)(2,1)S(1)} %collective-permute-done.up_ref, bf16[1,512,1024]{2,1,0:T(8,128)(2,1)S(1)} %collective-permute-done.1.down_ref), custom_call_target="tpu_custom_call" | custom-call | flops 805306368 | bytes 6000000 | tf_op jit(solution)/shard_map/pallas_call | solution.py:35
  54.7 11.7 %all_to_all.26.parts_ref = bf16[4,384,256]{2,1,0:T(8,128)(2,1)S(1)} all-to-all(bf16[4,384,256]{2,1,0:T(8,128)(2,1)S(1)} %shard_map.88), channel_id=1, replica_groups={{256,384,0,128},{257,385,1,129},{258,386,2,130},{259,387,3,131},{260,38..., dimensions={0} | all-to-all | bytes 1572864 | tf_op jit(solution)/shard_map/all_to_all | solution.py:216
  66.5 0.3 shard_map.89
  66.7 18.5 %all_to_all.27 = bf16[64,8,256]{2,1,0:T(8,128)(2,1)S(1)} all-to-all(bf16[64,8,256]{2,1,0:T(8,128)(2,1)S(1)} %bitcast.12), channel_id=1, replica_groups={{76,78,80,82,84,86,88,90,92,94,96,98,100,102,104,106,108,110,112,114,11..., dimensions={0} | all-to-all | bytes 524288 | tf_op jit(solution)/shard_map/all_to_all | solution.py:216
  85.2 0.8 shard_map.90
  (4 shorter events, 0.0 us)
Async XLA Ops:
  0.0 0.7 copy-start.2
  0.7 7.0 %copy-start.5 = (s32[3,16,2]{1,2,0:T(2,128)S(1)}, s32[3,16,2]{1,2,0:T(2,128)}, u32[]{:S(2)}) copy-start(s32[3,16,2]{1,2,0:T(2,128)} %param.14) | copy-start | bytes 1156
  0.7 7.0 %copy-start.6 = (f32[3,16,2]{1,2,0:T(2,128)S(1)}, f32[3,16,2]{1,2,0:T(2,128)}, u32[]{:S(2)}) copy-start(f32[3,16,2]{1,2,0:T(2,128)} %param.15) | copy-start | bytes 1156
  0.7 7.0 %copy-start.7 = (s32[3,16]{1,0:T(4,128)S(1)}, s32[3,16]{1,0:T(4,128)}, u32[]{:S(2)}) copy-start(s32[3,16]{1,0:T(4,128)} %parents_ref.1) | copy-start | bytes 580
  1.4 8.9 %all-to-all-start = ((bf16[4,48,256]{2,1,0:T(8,128)(2,1)}), bf16[4,48,256]{2,1,0:T(8,128)(2,1)S(1)}, u32[]{:S(2)}, u32[]{:S(2)}) async-start(bf16[4,48,256]{2,1,0:T(8,128)(2,1)} %shard_map.82), calls=%async_computation | async-start | bytes 196608 | tf_op jit(solution)/shard_map/all_to_all | solution.py:216
  7.7 2.6 %copy-start = (bf16[1024,3,256]{2,0,1:T(8,128)(2,1)S(1)}, bf16[1024,3,256]{2,0,1:T(8,128)(2,1)}, u32[]{:S(2)}) copy-start(bf16[1024,3,256]{2,0,1:T(8,128)(2,1)} %param.10) | copy-start | bytes 4718596
  7.7 2.6 %copy-start.1 = (bf16[16,2,64,256]{3,2,1,0:T(8,128)(2,1)S(1)}, bf16[16,2,64,256]{3,2,1,0:T(8,128)(2,1)}, u32[]{:S(2)}) copy-start(bf16[16,2,64,256]{3,2,1,0:T(8,128)(2,1)} %cache_ref.1) | copy-start | bytes 3145732
  7.7 2.5 %copy-start.3 = (bf16[3,16,256]{2,1,0:T(8,128)(2,1)S(1)}, bf16[3,16,256]{2,1,0:T(8,128)(2,1)}, u32[]{:S(2)}) copy-start(bf16[3,16,256]{2,1,0:T(8,128)(2,1)} %param.8) | copy-start | bytes 73732
  37.4 13.7 %all-to-all-start.2 = ((bf16[4,384,256]{2,1,0:T(8,128)(2,1)}), bf16[4,384,256]{2,1,0:T(8,128)(2,1)S(1)}, u32[]{:S(2)}, u32[]{:S(2)}) async-start(bf16[4,384,256]{2,1,0:T(8,128)(2,1)} %shard_map.85), calls=%async_computation.2 | async-start | bytes 1572864 | tf_op jit(solution)/shard_map/all_to_all | solution.py:216
  43.8 9.9 %collective-permute-start = (bf16[1,1024,512]{2,1,0:T(8,128)(2,1)}, bf16[1,1024,512]{2,1,0:T(8,128)(2,1)S(1)}, u32[]{:S(2)}, u32[]{:S(2)}) collective-permute-start(bf16[1,1024,512]{2,1,0:T(8,128)(2,1)} %up_hbm.1), channel_id=1, source_target_pairs={{0,1},{1,0},{2,3},{3,2},{4,5},{5,4},{6,7},{7,6},{8,9},{9,8},{10,11... | collective-permute-start | bytes 3145736 | tf_op jit(solution)/shard_map/ppermute | solution.py:223
  45.7 8.0 %collective-permute-start.1 = (bf16[1,512,1024]{2,1,0:T(8,128)(2,1)}, bf16[1,512,1024]{2,1,0:T(8,128)(2,1)S(1)}, u32[]{:S(2)}, u32[]{:S(2)}) collective-permute-start(bf16[1,512,1024]{2,1,0:T(8,128)(2,1)} %down_ref.1), channel_id=1, source_target_pairs={{0,1},{1,0},{2,3},{3,2},{4,5},{5,4},{6,7},{7,6},{8,9},{9,8},{10,11... | collective-permute-start | bytes 3145736 | tf_op jit(solution)/shard_map/ppermute | solution.py:224
  51.1 1.5 %copy-start.4 = (bf16[1,512,1024]{2,1,0:T(8,128)(2,1)S(1)}, bf16[1,512,1024]{2,1,0:T(8,128)(2,1)}, u32[]{:S(2)}) copy-start(bf16[1,512,1024]{2,1,0:T(8,128)(2,1)} %down_ref.1) | copy-start | bytes 3145732

commit v7 on v6

--- a/solution.py
+++ b/solution.py
@@ -208,7 +208,7 @@
     slots = experts * used
     shape = jax.ShapeDtypeStruct
 
-    first_expert = experts // 2 + 6
+    first_expert = experts // 2 + 3
     order = [[(p + first_expert) % experts for p in range(experts)]]
 
     def exchange(values, axis):

time: 86.6 us -> 88.9 us (1.027)
  the two profiles are of different devices: /device:TPU:8 before, /device:TPU:4 now
where the time goes in v7:
time: 88.9 us; the launch traced here: 88.4 us
  blocking collectives  53.4 us (60%)
  starting transfers between devices  15 us (17%)
  waiting for transfers between devices  10.8 us (12%)
  Pallas kernels  8.11 us (9%)
  local copies, waits for them, and re-layouts  0.98 us (1%)
    all_to_all x3, blocking collectives, exchange(): lax.all_to_all(values, axis, split_axis=0, concat_axis=0, tiled=True, axi...  53.4 us
    all_to_all x2, waiting for transfers between devices, exchange(): lax.all_to_all(values, axis, split_axis=0, concat_axis=0, tiled=True, axi...  10.8 us
    all_to_all x2, starting transfers between devices, exchange(): lax.all_to_all(values, axis, split_axis=0, concat_axis=0, tiled=True, axi...  10.6 us
    pallas_call x9, Pallas kernels, call(): pl.pallas_call(kernel, out_shape=outs, in_specs=[pl.BlockSpec(memory_spac...  8.11 us
    ppermute x1, starting transfers between devices, shards(): down_other = lax.ppermute(w_down, 'core', swap)  2.41 us
    ppermute x1, starting transfers between devices, shards(): up_other = lax.ppermute(w_up, 'core', swap)  1.92 us
  transfers between devices with their start and end apart: 4, of which 2 were waited for; matrix products, arithmetic and copies ran while one was open for 0% of the time, Pallas kernels for 3%

profile of v7, /device:TPU:4, one launch (start us, length us, event | category | flops | bytes accessed | tf_op | source)
XLA Modules:
  0.0 88.4 jit_solution(14039493481793825352)
XLA Ops:
  0.0 0.0 copy-start.2
  0.0 0.7 copy-done.2
  0.7 0.6 shard_map.82
  1.4 7.1 %all-to-all-start = ((bf16[4,48,256]{2,1,0:T(8,128)(2,1)}), bf16[4,48,256]{2,1,0:T(8,128)(2,1)S(1)}, u32[]{:S(2)}, u32[]{:S(2)}) async-start(bf16[4,48,256]{2,1,0:T(8,128)(2,1)} %shard_map.82), calls=%async_computation | async-start | bytes 196608 | tf_op jit(solution)/shard_map/all_to_all | solution.py:216
  8.5 0.0 copy-done.5
  8.5 0.0 copy-done.6
  8.5 0.0 copy-done.7
  8.6 0.0 copy-start
  8.6 0.0 copy-start.1
  8.6 0.0 copy-start.3
  8.6 0.7 shard_map.83
  9.3 5.0 %all-to-all-done.gathered_ref = bf16[4,48,256]{2,1,0:T(8,128)(2,1)S(1)} async-done(((bf16[4,48,256]{2,1,0:T(8,128)(2,1)}), bf16[4,48,256]{2,1,0:T(8,128)(2,1)S(1)}, u32[]{:S(2)}, u32[]{:S(2)}) %all-to-all-start) | async-done | bytes 98336 | tf_op jit(solution)/shard_map/all_to_all | solution.py:216
  14.3 0.0 copy-done
  14.3 0.0 copy-done.1
  14.3 0.0 copy-done.3
  14.4 1.2 %shard_map.84 = (bf16[48,256]{1,0:T(8,128)(2,1)S(1)}, bf16[512,256]{1,0:T(8,128)(2,1)S(1)}) custom-call(bf16[4,48,256]{2,1,0:T(8,128)(2,1)S(1)} %all-to-all-done.gathered_ref, bf16[48,256]{1,0:T(8,128)(2,1)S(1)} %bitcast.15, bf16[3,1024,256]{2,1,0:T(8,128)(2,1)S(1)} %bitcast.9, bf16[16,2,64,256]{3,2,1,0:T(8,128)(2,1)S(1)} %copy-done.1, ...), custom_call_target="tpu_custom_call" | custom-call | flops 75497472 | bytes 3000000 | tf_op jit(solution)/shard_map/pallas_call | solution.py:35
  15.6 23.0 %all_to_all.25 = bf16[64,8,256]{2,1,0:T(8,128)(2,1)S(1)} all-to-all(bf16[64,8,256]{2,1,0:T(8,128)(2,1)S(1)} %bitcast.13), channel_id=1, replica_groups={{70,72,74,76,78,80,82,84,86,88,90,92,94,96,98,100,102,104,106,108,110,1..., dimensions={0} | all-to-all | bytes 524288 | tf_op jit(solution)/shard_map/all_to_all | solution.py:216
  38.6 1.1 %shard_map.85 = bf16[4,384,256]{2,1,0:T(8,128)(2,1)} custom-call(bf16[512,256]{1,0:T(8,128)(2,1)S(1)} %bitcast.11), custom_call_target="tpu_custom_call" | custom-call | tf_op jit(solution)/shard_map/pallas_call | solution.py:35
  39.7 3.5 %all-to-all-start.2 = ((bf16[4,384,256]{2,1,0:T(8,128)(2,1)}), bf16[4,384,256]{2,1,0:T(8,128)(2,1)S(1)}, u32[]{:S(2)}, u32[]{:S(2)}) async-start(bf16[4,384,256]{2,1,0:T(8,128)(2,1)} %shard_map.85), calls=%async_computation.2 | async-start | bytes 1572864 | tf_op jit(solution)/shard_map/all_to_all | solution.py:216
  43.2 1.9 %collective-permute-start = (bf16[1,1024,512]{2,1,0:T(8,128)(2,1)}, bf16[1,1024,512]{2,1,0:T(8,128)(2,1)S(1)}, u32[]{:S(2)}, u32[]{:S(2)}) collective-permute-start(bf16[1,1024,512]{2,1,0:T(8,128)(2,1)} %up_hbm.1), channel_id=1, source_target_pairs={{0,1},{1,0},{2,3},{3,2},{4,5},{5,4},{6,7},{7,6},{8,9},{9,8},{10,11... | collective-permute-start | bytes 3145736 | tf_op jit(solution)/shard_map/ppermute | solution.py:223
  45.1 2.4 %collective-permute-start.1 = (bf16[1,512,1024]{2,1,0:T(8,128)(2,1)}, bf16[1,512,1024]{2,1,0:T(8,128)(2,1)S(1)}, u32[]{:S(2)}, u32[]{:S(2)}) collective-permute-start(bf16[1,512,1024]{2,1,0:T(8,128)(2,1)} %down_ref.1), channel_id=1, source_target_pairs={{0,1},{1,0},{2,3},{3,2},{4,5},{5,4},{6,7},{7,6},{8,9},{9,8},{10,11... | collective-permute-start | bytes 3145736 | tf_op jit(solution)/shard_map/ppermute | solution.py:224
  47.5 5.8 %all-to-all-done.2.slots_ref = bf16[4,384,256]{2,1,0:T(8,128)(2,1)S(1)} async-done(((bf16[4,384,256]{2,1,0:T(8,128)(2,1)}), bf16[4,384,256]{2,1,0:T(8,128)(2,1)S(1)}, u32[]{:S(2)}, u32[]{:S(2)}) %all-to-all-start.2) | async-done | bytes 786464 | tf_op jit(solution)/shard_map/all_to_all | solution.py:216
  53.3 1.3 %shard_map.86 = (bf16[384,1024]{1,0:T(8,128)(2,1)S(1)}, bf16[1,1024,512]{2,1,0:T(8,128)(2,1)S(1)}) custom-call(bf16[4,384,256]{2,1,0:T(8,128)(2,1)S(1)} %all-to-all-done.2.slots_ref, bf16[1,1024,512]{2,1,0:T(8,128)(2,1)} %up_hbm.1), custom_call_target="tpu_custom_call" | custom-call | flops 1000000000 | bytes 10000000 | tf_op jit(solution)/shard_map/pallas_call | solution.py:35
  54.6 0.2 copy-done.4
  54.9 1.0 %shard_map.87.sum_ref = f32[384,1024]{1,0:T(8,128)S(1)} custom-call(bf16[384,1024]{1,0:T(8,128)(2,1)S(1)} %get-tuple-element.17.normed_ref, bf16[1,1024,512]{2,1,0:T(8,128)(2,1)S(1)} %get-tuple-element.18.up_ref, bf16[1,512,1024]{2,1,0:T(8,128)(2,1)S(1)} %copy-done.4), custom_call_target="tpu_custom_call" | custom-call | flops 99999997952 | bytes 10000000 | tf_op jit(solution)/shard_map/pallas_call | solution.py:35
  55.9 0.0 collective-permute-done.up_ref
  55.9 0.0 collective-permute-done.1.down_ref
  55.9 1.0 %shard_map.88 = bf16[4,384,256]{2,1,0:T(8,128)(2,1)S(1)} custom-call(bf16[384,1024]{1,0:T(8,128)(2,1)S(1)} %get-tuple-element.17.normed_ref, f32[384,1024]{1,0:T(8,128)S(1)} %shard_map.87.sum_ref, bf16[1,1024,512]{2,1,0:T(8,128)(2,1)S(1)} %collective-permute-done.up_ref, bf16[1,512,1024]{2,1,0:T(8,128)(2,1)S(1)} %collective-permute-done.1.down_ref), custom_call_target="tpu_custom_call" | custom-call | flops 805306368 | bytes 6000000 | tf_op jit(solution)/shard_map/pallas_call | solution.py:35
  56.9 11.9 %all_to_all.26.parts_ref = bf16[4,384,256]{2,1,0:T(8,128)(2,1)S(1)} all-to-all(bf16[4,384,256]{2,1,0:T(8,128)(2,1)S(1)} %shard_map.88), channel_id=1, replica_groups={{256,384,0,128},{257,385,1,129},{258,386,2,130},{259,387,3,131},{260,38..., dimensions={0} | all-to-all | bytes 1572864 | tf_op jit(solution)/shard_map/all_to_all | solution.py:216
  68.8 0.3 shard_map.89
  69.1 18.5 %all_to_all.27 = bf16[64,8,256]{2,1,0:T(8,128)(2,1)S(1)} all-to-all(bf16[64,8,256]{2,1,0:T(8,128)(2,1)S(1)} %bitcast.12), channel_id=1, replica_groups={{70,72,74,76,78,80,82,84,86,88,90,92,94,96,98,100,102,104,106,108,110,1..., dimensions={0} | all-to-all | bytes 524288 | tf_op jit(solution)/shard_map/all_to_all | solution.py:216
  87.6 0.8 shard_map.90
  (4 shorter events, 0.0 us)
Async XLA Ops:
  0.0 0.7 copy-start.2
  0.7 7.8 %copy-start.5 = (s32[3,16,2]{1,2,0:T(2,128)S(1)}, s32[3,16,2]{1,2,0:T(2,128)}, u32[]{:S(2)}) copy-start(s32[3,16,2]{1,2,0:T(2,128)} %param.14) | copy-start | bytes 1156
  0.7 7.8 %copy-start.6 = (f32[3,16,2]{1,2,0:T(2,128)S(1)}, f32[3,16,2]{1,2,0:T(2,128)}, u32[]{:S(2)}) copy-start(f32[3,16,2]{1,2,0:T(2,128)} %param.15) | copy-start | bytes 1156
  0.7 7.8 %copy-start.7 = (s32[3,16]{1,0:T(4,128)S(1)}, s32[3,16]{1,0:T(4,128)}, u32[]{:S(2)}) copy-start(s32[3,16]{1,0:T(4,128)} %parents_ref.1) | copy-start | bytes 580
  1.4 13.0 %all-to-all-start = ((bf16[4,48,256]{2,1,0:T(8,128)(2,1)}), bf16[4,48,256]{2,1,0:T(8,128)(2,1)S(1)}, u32[]{:S(2)}, u32[]{:S(2)}) async-start(bf16[4,48,256]{2,1,0:T(8,128)(2,1)} %shard_map.82), calls=%async_computation | async-start | bytes 196608 | tf_op jit(solution)/shard_map/all_to_all | solution.py:216
  8.6 5.8 %copy-start = (bf16[1024,3,256]{2,0,1:T(8,128)(2,1)S(1)}, bf16[1024,3,256]{2,0,1:T(8,128)(2,1)}, u32[]{:S(2)}) copy-start(bf16[1024,3,256]{2,0,1:T(8,128)(2,1)} %param.10) | copy-start | bytes 4718596
  8.6 5.8 %copy-start.1 = (bf16[16,2,64,256]{3,2,1,0:T(8,128)(2,1)S(1)}, bf16[16,2,64,256]{3,2,1,0:T(8,128)(2,1)}, u32[]{:S(2)}) copy-start(bf16[16,2,64,256]{3,2,1,0:T(8,128)(2,1)} %cache_ref.1) | copy-start | bytes 3145732
  8.6 5.8 %copy-start.3 = (bf16[3,16,256]{2,1,0:T(8,128)(2,1)S(1)}, bf16[3,16,256]{2,1,0:T(8,128)(2,1)}, u32[]{:S(2)}) copy-start(bf16[3,16,256]{2,1,0:T(8,128)(2,1)} %param.8) | copy-start | bytes 73732
  39.7 13.6 %all-to-all-start.2 = ((bf16[4,384,256]{2,1,0:T(8,128)(2,1)}), bf16[4,384,256]{2,1,0:T(8,128)(2,1)S(1)}, u32[]{:S(2)}, u32[]{:S(2)}) async-start(bf16[4,384,256]{2,1,0:T(8,128)(2,1)} %shard_map.85), calls=%async_computation.2 | async-start | bytes 1572864 | tf_op jit(solution)/shard_map/all_to_all | solution.py:216
  43.2 12.7 %collective-permute-start = (bf16[1,1024,512]{2,1,0:T(8,128)(2,1)}, bf16[1,1024,512]{2,1,0:T(8,128)(2,1)S(1)}, u32[]{:S(2)}, u32[]{:S(2)}) collective-permute-start(bf16[1,1024,512]{2,1,0:T(8,128)(2,1)} %up_hbm.1), channel_id=1, source_target_pairs={{0,1},{1,0},{2,3},{3,2},{4,5},{5,4},{6,7},{7,6},{8,9},{9,8},{10,11... | collective-permute-start | bytes 3145736 | tf_op jit(solution)/shard_map/ppermute | solution.py:223
  45.1 10.8 %collective-permute-start.1 = (bf16[1,512,1024]{2,1,0:T(8,128)(2,1)}, bf16[1,512,1024]{2,1,0:T(8,128)(2,1)S(1)}, u32[]{:S(2)}, u32[]{:S(2)}) collective-permute-start(bf16[1,512,1024]{2,1,0:T(8,128)(2,1)} %down_ref.1), channel_id=1, source_target_pairs={{0,1},{1,0},{2,3},{3,2},{4,5},{5,4},{6,7},{7,6},{8,9},{9,8},{10,11... | collective-permute-start | bytes 3145736 | tf_op jit(solution)/shard_map/ppermute | solution.py:224
  53.3 1.5 %copy-start.4 = (bf16[1,512,1024]{2,1,0:T(8,128)(2,1)S(1)}, bf16[1,512,1024]{2,1,0:T(8,128)(2,1)}, u32[]{:S(2)}) copy-start(bf16[1,512,1024]{2,1,0:T(8,128)(2,1)} %down_ref.1) | copy-start | bytes 3145732
